TPU v7x, 256 devices: a whole 4x4x8 slice. The times are simulated.
256 devices in a mesh: prow: 8 (over z_hi, x), pcol: 32 (over y, z_lo, core).
Axes of the slice: x: 4, y: 4, z: 8 (z_hi: 2, z_lo: 4; z = z_hi * 4 + z_lo), core: 2. Of those that a mesh axis runs over, the one named last changes fastest.
Arguments:
- ancestor_inverse: bfloat16 [12288, 12288], P('prow', 'pcol'), may hold values from -0.0546875 to 0.0546875
- factor_panel: bfloat16 [12288, 4096], P('prow', 'pcol'), may hold values from -0.67578125 to 0.67578125
- pivot_inverse: float32 [512, 4096], P('prow', 'pcol'), may hold values from -6 to 6
- sn_size: int32 [8], replicated, may hold values from 128 to 512, as said below
- anc_list: int32 [8, 48], replicated, may hold values from 0 to 95, all different within a row
Outputs:
- ainv_cols: bfloat16 [4096, 12288], P('pcol', 'prow')
- diag_inverse: float32 [512, 4096], P('prow', 'pcol')
Inputs may be any that keep to these rules, and one draw needn't show every extreme that they name: `sn_size`: every supernode has between 128 and 512 live columns; some supernode has exactly 512 and some exactly 128. `anc_list`: each row lists 48 distinct ancestor blocks; every block is listed by some supernode.
All inputs are finite; a program needn't handle non-finite values.
Results may differ from a plain program's by a relative error of at most 0.0018.
Values may be sent and summed in bfloat16 or wider, within the bound.
A program may use at most 128 MiB of HBM per device.

v0:
```python
import jax
import jax.numpy as jnp
from jax import lax
from jax.sharding import PartitionSpec as P

AB = 128
W = 512
SN = 8


def broadcast(block, axis, owner):
    block = jnp.where(lax.axis_index(axis) == owner, block, jnp.zeros_like(block))
    return lax.psum(block, axis)


def local_masks(
    sn_size,
    anc_list,
    block_count,
    row_start,
    row_count,
    col_start,
    col_count,
    lead_start,
    lead_count,
):
    blocks = jnp.arange(block_count, dtype=jnp.int32)
    block_live = jnp.any(anc_list[:, :, None] == blocks[None, None, :], axis=1).astype(jnp.float32)
    row_ids = (row_start + jnp.arange(row_count, dtype=jnp.int32)) // AB
    row_pick = (row_ids[:, None] == blocks[None, :]).astype(jnp.float32)
    row_live = jnp.dot(row_pick, block_live.T)
    cols = col_start + jnp.arange(col_count, dtype=jnp.int32)
    owner = cols // W
    owner_pick = (owner[:, None] == jnp.arange(SN, dtype=jnp.int32)[None, :]).astype(jnp.float32)
    size_col = jnp.sum(owner_pick * sn_size[None, :].astype(jnp.float32), axis=1)
    col_live = ((cols % W).astype(jnp.float32) < size_col).astype(jnp.float32)
    panel_live = jnp.dot(row_live, owner_pick.T) * col_live[None, :]
    lead = (lead_start + jnp.arange(lead_count, dtype=jnp.int32)).astype(jnp.float32)
    diag_keep = (lead[:, None] < size_col[None, :]).astype(jnp.float32) * col_live[None, :]
    return (panel_live, diag_keep)


def per_device(ancestor_inverse, factor_panel, pivot_inverse, sn_size, anc_list):
    row_count = factor_panel.shape[0]
    col_count = factor_panel.shape[1]
    inv_cols = ancestor_inverse.shape[1]
    lead_count = pivot_inverse.shape[0]
    block_count = row_count * lax.axis_size("prow") // AB
    prow_at = lax.axis_index("prow")
    pcol_at = lax.axis_index("pcol")
    row_start = prow_at * row_count
    col_start = pcol_at * col_count
    panel_live, diag_keep = local_masks(
        sn_size,
        anc_list,
        block_count,
        row_start,
        row_count,
        col_start,
        col_count,
        prow_at * lead_count,
        lead_count,
    )
    lhat = (factor_panel.astype(jnp.float32) * panel_live).astype(jnp.bfloat16)
    row_full = lax.all_gather(lhat, "pcol", axis=1, tiled=True)
    inv_start = pcol_at * inv_cols
    root = inv_start // row_count
    offset = inv_start % row_count
    own_rows = lax.dynamic_slice_in_dim(row_full, offset, inv_cols, 0)
    col_rows = broadcast(own_rows, "prow", root)
    summed = lax.psum_scatter(
        lax.dot_general(
            col_rows, ancestor_inverse, (((0,), (1,)), ((), ())), preferred_element_type=jnp.float32
        ),
        "pcol",
        scatter_dimension=0,
        tiled=True,
    )
    ainv_local = (-(summed * panel_live.T)).astype(jnp.bfloat16)
    owner_first = col_start // W * W
    lead_panel = lax.dynamic_slice_in_dim(row_full, owner_first, W, 1)
    partial_corr = lax.dot_general(
        lead_panel, ainv_local, (((0,), (1,)), ((), ())), preferred_element_type=jnp.float32
    )
    corr = lax.psum_scatter(partial_corr, "prow", scatter_dimension=0, tiled=True)
    diag = (pivot_inverse - corr) * diag_keep
    return (ainv_local, diag)


def solution(mesh):
    return jax.shard_map(
        per_device,
        mesh=mesh,
        in_specs=(P("prow", "pcol"), P("prow", "pcol"), P("prow", "pcol"), P(), P()),
        out_specs=(P("pcol", "prow"), P("prow", "pcol")),
        check_vma=False,
    )
```

profile of v0, /device:TPU:57, one launch (start us, length us, event | category | flops | bytes accessed | tf_op | source)
XLA Modules:
  0.0 666.1 jit_solution(3919391637142248006)
XLA Ops:
  7.2 0.0 copy-start
  7.2 0.0 all-gather.2.cloned.1.call-start
  7.2 0.7 convert_element_type.40
  8.0 0.1 select_reduce_fusion
  8.1 0.8 fusion.8
  8.9 2.3 multiply_convert_fusion
  11.2 0.0 all-gather.2.cloned.1.call-update
  11.2 0.0 all-reduce.2.cloned.1.call-start
  11.3 106.9 %all-gather.2.cloned.1.call-done = bf16[1536,4096]{1,0:T(8,128)(2,1)} async-done(((bf16[1536,128]{1,0:T(8,128)(2,1)}), bf16[1536,4096]{1,0:T(8,128)(2,1)}) %all-gather.2.cloned.1.call-update) | async-done | bytes 12582928 | tf_op jit(solution)/shard_map/all_gather | solution.py:65
  118.2 4.6 dynamic-slice_select_fusion
  122.8 0.0 all-reduce.2.cloned.1.call-update
  122.8 0.0 reduce-scatter.3.cloned.1.call-start
  122.8 160.6 %all-reduce.2.cloned.1.call-done = bf16[384,4096]{1,0:T(8,128)(2,1)} async-done(((bf16[384,4096]{1,0:T(8,128)(2,1)}), bf16[384,4096]{1,0:T(8,128)(2,1)}) %all-reduce.2.cloned.1.call-update) | async-done | bytes 3145744 | tf_op jit(solution)/shard_map/psum | solution.py:13
  283.5 0.0 copy-done
  283.5 13.5 %fusion.15 = f32[4096,1536]{0,1:T(8,128)} fusion(bf16[1536,384]{1,0:T(8,128)(2,1)S(1)} %copy-done, bf16[384,4096]{1,0:T(8,128)(2,1)} %all-reduce.2.cloned.1.call-done), kind=kOutput, calls=%fused_computation.36 | convolution fusion | flops 4831838208 | bytes 29491200 | tf_op jit(solution)/shard_map/dot_general | solution.py:72
  297.0 0.0 reduce-scatter.3.cloned.1.call-update
  297.0 0.0 copy-start.1
  297.0 0.0 reduce-scatter.5.cloned.1.call-start
  297.1 276.6 %reduce-scatter.3.cloned.1.call-done = f32[128,1536]{0,1:T(8,128)} async-done(((f32[4096,1536]{0,1:T(8,128)}), f32[128,1536]{0,1:T(8,128)}) %reduce-scatter.3.cloned.1.call-update) | async-done | bytes 786448 | tf_op jit(solution)/shard_map/reduce_scatter | solution.py:71
  573.7 1.2 fusion.5
  575.0 2.7 fusion
  577.7 0.0 reduce-scatter.5.cloned.1.call-update
  577.7 0.9 copy.10
  578.7 79.5 %reduce-scatter.5.cloned.1.call-done = f32[64,128]{1,0:T(8,128)} async-done(((f32[512,128]{1,0:T(8,128)}), f32[64,128]{1,0:T(8,128)}) %reduce-scatter.5.cloned.1.call-update) | async-done | bytes 32784 | tf_op jit(solution)/shard_map/reduce_scatter | solution.py:85
  658.1 0.0 copy-done.1
  658.1 1.4 select_multiply_fusion
  (4 shorter events, 0.0 us)
Async XLA Ops:
  7.2 276.3 %copy-start = (bf16[1536,384]{1,0:T(8,128)(2,1)S(1)}, bf16[1536,384]{1,0:T(8,128)(2,1)}, u32[]{:S(2)}) copy-start(bf16[1536,384]{1,0:T(8,128)(2,1)} %param.5) | copy-start | bytes 3538948
  7.2 111.0 %all-gather.2.cloned.1.call-start = ((), (), s32[]{:S(2)}) async-start(), calls=%async_computation.2 | async-start | bytes 12976128 | tf_op jit(solution)/shard_map/all_gather | solution.py:65
  11.2 272.3 %all-reduce.2.cloned.1.call-start = ((), (), s32[]{:S(2)}) async-start(), calls=%async_computation.3 | async-start | bytes 6291456 | tf_op jit(solution)/shard_map/psum | solution.py:13
  122.8 451.0 %reduce-scatter.3.cloned.1.call-start = ((), (), s32[]{:S(2)}) async-start(), calls=%async_computation.4 | async-start | bytes 25952256 | tf_op jit(solution)/shard_map/reduce_scatter | solution.py:71
  297.0 361.1 %copy-start.1 = (f32[64,128]{1,0:T(8,128)S(1)}, f32[64,128]{1,0:T(8,128)}, u32[]{:S(2)}) copy-start(f32[64,128]{1,0:T(8,128)} %param.7) | copy-start | bytes 98308
  297.0 361.1 %reduce-scatter.5.cloned.1.call-start = ((), (), s32[]{:S(2)}) async-start(), calls=%async_computation.5 | async-start | bytes 294912 | tf_op jit(solution)/shard_map/reduce_scatter | solution.py:85
Sparse Core Ops, SparseCore 0:
  11.3 106.8 all-gather.1
  122.9 160.5 all-reduce.1
  297.2 276.5 reduce-scatter.2
  577.8 80.2 reduce-scatter.4
where the time goes:
time: 670 us; the launch traced here: 666 us
  waiting for transfers between devices  624 us (93%)
  matrix products  18.5 us (3%)
  between operations  13.9 us (2%)
  other arithmetic  8.93 us (1%)
    reduce_scatter x1, waiting for transfers between devices, per_device(): lax.psum_scatter(lax.dot_general(col_rows, ancestor_inverse, (((0,), (1,)...  277 us
    psum x1, waiting for transfers between devices, broadcast(): return lax.psum(block, axis)  161 us
    all_gather x1, waiting for transfers between devices, per_device(): row_full = lax.all_gather(lhat, 'pcol', axis=1, tiled=True)  107 us
    reduce_scatter x1, waiting for transfers between devices, per_device(): lax.psum_scatter(partial_corr, 'prow', scatter_dimension=0, tiled=True)  79.5 us
    dot_general x1, matrix products, per_device(): lax.dot_general(col_rows, ancestor_inverse, (((0,), (1,)), ((), ())), pre...  13.5 us
  transfers between devices with their start and end apart: 4, of which 4 were waited for; matrix products, arithmetic and copies ran while one was open for 0% of the time, Pallas kernels for 0%

commit v1 on v0

v1 whole, which is shorter than its diff:
```python
import jax
import jax.numpy as jnp
from jax import lax
from jax.experimental import pallas as pl
from jax.experimental.pallas import tpu as pltpu
from jax.sharding import PartitionSpec as P

AB = 128
W = 512
MESH = pl.DeviceIdType.MESH
MCH = 4


def kernel(
    a_ref, l_ref, piv_ref, sn_ref, anc_ref, out_ref, diag_ref,
    abuf, lhat, lbuf, lead, live, acc, cown, csend, crecv, abf, corr, drecv,
    ld_sem, lz_s, l_r, lx_s, a_s, a_r, ab_r, c_s, c_r, h_s, h_r, d_s, d_r,
):
    rows = l_ref.shape[0]
    mrows = rows // MCH
    half = rows // 2
    kw = a_ref.shape[1]
    tiles = mrows // AB
    p = lax.axis_index("prow")
    q = lax.axis_index("pcol")
    x, zh = p % 4, p // 4
    y, zl, c = q // 8, (q // 2) % 4, q % 2
    z = zh * 4 + zl
    k = q // 4

    def dev(x_, y_, z_, c_):
        return ((z_ // 4) * 4 + x_, y_ * 8 + (z_ % 4) * 2 + c_)

    def at_x(d):
        return dev((x + d) % 4, y, z, c)

    def at_y(d):
        return dev(x, (y + d) % 4, z, c)

    def at_z(z_):
        return dev(x, y, z_, c)

    sib = dev(x, y, z, 1 - c)

    def rcopy(src, dst, ssem, rsem, device):
        return pltpu.make_async_remote_copy(
            src_ref=src, dst_ref=dst, send_sem=ssem, recv_sem=rsem,
            device_id=device, device_id_type=MESH)

    barrier = pltpu.get_barrier_semaphore()
    partners = [at_z((z + d) % 8) for d in range(1, 8)]
    partners += [dev((x + d) % 4, y, ((zh + e) % 2) * 4 + zl, c)
                 for d in range(1, 4) for e in range(2)]
    partners += [at_y(1), at_y(3), sib]
    for partner in partners:
        pl.semaphore_signal(barrier, inc=1, device_id=partner, device_id_type=MESH)

    def mchunk(m):
        return pl.ds(m * mrows, mrows)

    def ablk(y_, c_, r):
        return abuf.at[y_, r, pl.ds(pl.multiple_of(c_ * kw, 128), kw)]

    def load(m):
        r = mchunk(m)
        return pltpu.make_async_copy(a_ref.at[r, :], ablk(y, c, r), ld_sem.at[m])

    for m in range(MCH):
        load(m).start()

    ids = p * (rows // AB) + lax.broadcasted_iota(jnp.int32, (16, anc_ref.shape[1]), 0)
    hit = jnp.where(ids == anc_ref[pl.ds(k, 1), :], 1.0, 0.0)
    row_live = jnp.max(hit, axis=1, keepdims=True)
    cols = (q % 4) * AB + lax.broadcasted_iota(jnp.int32, (1, AB), 1)
    col_live = jnp.where(cols < sn_ref[k], 1.0, 0.0)
    live[...] = row_live * col_live
    for b in range(rows // AB):
        r = pl.ds(b * AB, AB)
        lhat[r, :] = (l_ref[r, :].astype(jnp.float32) * live[b:b + 1, :]).astype(jnp.bfloat16)

    pl.semaphore_wait(barrier, len(partners))

    def lslot(xs, zs):
        lane = ((zs % 4 - zl + 4) % 4) * AB
        return lbuf.at[(zs // 4) * 2 + xs, :, pl.ds(pl.multiple_of(lane, 128), AB)]

    def lsem(xs, zs):
        return l_r.at[xs * 8 + zs]

    zsends = []
    for hh in range(2):
        for e in range(2):
            tz = (x % 2) * 2 + hh
            to = e * 4 + tz
            lane = ((zl - tz + 4) % 4) * AB
            dst = lbuf.at[zh * 2 + x // 2, :, pl.ds(pl.multiple_of(lane, 128), AB)]
            src = lhat.at[pl.ds(hh * half, half), :]
            rem = rcopy(src, dst, lz_s.at[hh * 2 + e], lsem(x // 2, z), at_z(to))
            loc = pltpu.make_async_copy(src, dst, lsem(x // 2, z))
            zsends.append((to != z, rem))

            @pl.when(to != z)
            def _(rem=rem):
                rem.start()

            @pl.when(to == z)
            def _(loc=loc):
                loc.start()

    def a_own(m):
        r = mchunk(m)
        blk = ablk(y, c, r)
        return [rcopy(blk, blk, a_s.at[m, 0], a_r.at[m, 0], at_y(1)),
                rcopy(blk, blk, a_s.at[m, 1], a_r.at[m, 1], at_y(3)),
                rcopy(blk, blk, a_s.at[m, 2], ab_r.at[m, 0], sib)]

    hr = mrows // 2

    def a_fwd(m):
        lo, hi = pl.ds(m * mrows, hr), pl.ds(m * mrows + hr, hr)
        r = mchunk(m)
        ym, yp = (y + 3) % 4, (y + 1) % 4
        return [rcopy(ablk(ym, c, lo), ablk(ym, c, lo), a_s.at[m, 3], a_r.at[m, 2], at_y(1)),
                rcopy(ablk(yp, c, hi), ablk(yp, c, hi), a_s.at[m, 4], a_r.at[m, 3], at_y(3)),
                rcopy(ablk(ym, c, r), ablk(ym, c, r), a_s.at[m, 5], ab_r.at[m, 1], sib),
                rcopy(ablk(yp, c, r), ablk(yp, c, r), a_s.at[m, 6], ab_r.at[m, 2], sib)]

    def a_opp(m):
        lo, hi = pl.ds(m * mrows, hr), pl.ds(m * mrows + hr, hr)
        yo = (y + 2) % 4
        return [rcopy(ablk(yo, c, lo), ablk(yo, c, lo), a_s.at[m, 7], ab_r.at[m, 3], sib),
                rcopy(ablk(yo, c, hi), ablk(yo, c, hi), a_s.at[m, 8], ab_r.at[m, 4], sib)]

    def wait_into(ref, sem):
        pltpu.make_async_copy(ref, ref, sem).wait()

    for m in range(MCH):
        load(m).wait()
        for cp in a_own(m):
            cp.start()

    zmate = z + 1 - 2 * (z % 2)

    def hblk(zb, cb):
        return lead.at[:, pl.ds(pl.multiple_of(((zb % 2) * 2 + cb) * AB, 128), AB)]

    h_own = [rcopy(lhat, hblk(z, c), h_s.at[0], h_r.at[0], at_z(zmate)),
             rcopy(lhat, hblk(z, c), h_s.at[1], h_r.at[1], sib)]
    h_fwd = rcopy(hblk(zmate, c), hblk(zmate, c), h_s.at[2], h_r.at[2], sib)
    h_loc = pltpu.make_async_copy(lhat, hblk(z, c), h_s.at[3])
    h_loc.start()

    is_src = x % 2 == zl // 2
    order = [0, 1, 7, 2, 6, 3, 5, 4]

    def x_src(i):
        zs = (z + order[i]) % 8
        xs = x // 2
        return [rcopy(lslot(xs, zs), lslot(xs, zs), lx_s.at[i * 2 + n], lsem(xs, zs), at_x(d))
                for n, d in enumerate((1, 3))]

    def x_mid(i):
        zs = (z + order[i]) % 8
        xm, xp = ((x + 3) % 4) // 2, ((x + 1) % 4) // 2
        return (zs, xm, xp,
                rcopy(lslot(xm, zs), lslot(xm, zs), lx_s.at[i], lsem(xm, zs), at_x(1)),
                rcopy(lslot(xp, zs), lslot(xp, zs), lx_s.at[i], lsem(xp, zs), at_x(3)))

    for i in range(8):
        @pl.when(is_src)
        def _(i=i):
            zs = (z + order[i]) % 8
            wait_into(lslot(x // 2, zs), lsem(x // 2, zs))
            for cp in x_src(i):
                cp.start()

        @pl.when(jnp.logical_not(is_src))
        def _(i=i):
            zs, xm, xp, up, down = x_mid(i)
            wait_into(lslot(xm, zs), lsem(xm, zs))

            @pl.when(zs % 2 == 0)
            def _():
                up.start()

            wait_into(lslot(xp, zs), lsem(xp, zs))

            @pl.when(zs % 2 == 1)
            def _():
                down.start()

        if i % 2 == 1:
            m = i // 2
            r = mchunk(m)
            cps = a_fwd(m)
            wait_into(ablk((y + 3) % 4, c, r), a_r.at[m, 0])
            cps[0].start()
            cps[2].start()
            wait_into(ablk((y + 1) % 4, c, r), a_r.at[m, 1])
            cps[1].start()
            cps[3].start()
        if i == 5:
            for cp in h_own:
                cp.start()

    for i in range(8):
        @pl.when(is_src)
        def _(i=i):
            zs = (z + order[i]) % 8
            xo = 1 - x // 2
            wait_into(lslot(xo, zs), lsem(xo, zs))

    for m in range(MCH):
        yo = (y + 2) % 4
        cps = a_opp(m)
        wait_into(ablk(yo, c, pl.ds(m * mrows, hr)), a_r.at[m, 2])
        cps[0].start()
        wait_into(ablk(yo, c, pl.ds(m * mrows + hr, hr)), a_r.at[m, 3])
        cps[1].start()

    def c_copy(m, j):
        return rcopy(csend.at[m, j - 1], crecv.at[m, j - 1], c_s.at[m, j - 1], c_r.at[m, j - 1],
                     at_z(zh * 4 + (zl + j) % 4))

    @pl.loop(0, MCH)
    def _(m):
        r = pl.ds(pl.multiple_of(m * mrows, mrows), mrows)
        lo = pl.ds(pl.multiple_of(m * mrows, hr), hr)
        hi = pl.ds(pl.multiple_of(m * mrows + hr, hr), hr)
        oc = 1 - c
        wait_into(ablk(y, oc, r), ab_r.at[m, 0])
        wait_into(ablk((y + 3) % 4, oc, r), ab_r.at[m, 1])
        wait_into(ablk((y + 1) % 4, oc, r), ab_r.at[m, 2])
        wait_into(ablk((y + 2) % 4, oc, lo), ab_r.at[m, 3])
        wait_into(ablk((y + 2) % 4, oc, hi), ab_r.at[m, 4])
        acc[...] = jnp.dot(abuf[0, r, :], lbuf[0], preferred_element_type=jnp.float32)
        for yy in range(1, 4):
            acc[...] += jnp.dot(abuf[yy, r, :], lbuf[yy], preferred_element_type=jnp.float32)
        cown[r, :] = acc[:, 0:AB]
        for j in range(1, 4):
            for t in range(tiles):
                part = acc[t * AB:(t + 1) * AB, j * AB:(j + 1) * AB]
                top = jnp.max(jnp.abs(part), axis=0, keepdims=True)
                e = jnp.clip(jnp.floor(jnp.log2(jnp.maximum(top, 1e-30))) + 1.0, -90.0, 90.0)
                v = jnp.clip(jnp.round(part * jnp.exp2(15.0 - e)), -32767.0, 32767.0)
                csend[m, j - 1, t, 0:AB, :] = v.astype(jnp.int32).astype(jnp.int16)
                csend[m, j - 1, t, AB:AB + 16, :] = jnp.broadcast_to(
                    e.astype(jnp.int32), (16, AB)).astype(jnp.int16)
            c_copy(m, j).start()

    wait_into(hblk(zmate, c), h_r.at[0])
    h_fwd.start()
    h_loc.wait()
    wait_into(hblk(z, 1 - c), h_r.at[1])
    wait_into(hblk(zmate, 1 - c), h_r.at[2])

    corr[...] = jnp.zeros_like(corr)

    @pl.loop(0, MCH)
    def _(m):
        r = pl.ds(pl.multiple_of(m * mrows, mrows), mrows)
        for j in range(1, 4):
            wait_into(crecv.at[m, j - 1], c_r.at[m, j - 1])
        for t in range(tiles):
            at = pl.multiple_of(m * mrows + t * AB, AB)
            s = cown[pl.ds(at, AB), :]
            for j in range(1, 4):
                v = crecv[m, j - 1, t, 0:AB, :].astype(jnp.int32).astype(jnp.float32)
                e = crecv[m, j - 1, t, AB:AB + 16, :].astype(jnp.int32).astype(jnp.float32)
                s = s + v * jnp.exp2(e[0:1, :] - 15.0)
            s = -(s * live[pl.ds(m * tiles + t, 1), :])
            abf[t * AB:(t + 1) * AB, :] = s.astype(jnp.bfloat16)
            out_ref[:, pl.ds(at, AB)] = s.T.astype(jnp.bfloat16)
        corr[...] += lax.dot_general(
            lead[r, :], abf[...], (((0,), (0,)), ((), ())), preferred_element_type=jnp.float32)

    lrows = diag_ref.shape[0]

    def mine(p_):
        return pl.ds(pl.multiple_of(p_ * lrows, lrows), lrows)

    dcopies = []
    for d in range(1, 8):
        to = (p + d) % 8
        cp = rcopy(corr.at[mine(to), :], drecv.at[d - 1], d_s.at[d - 1], d_r.at[d - 1], (to, q))
        cp.start()
        dcopies.append(cp)
    total = corr[mine(p), :]
    for d in range(1, 8):
        wait_into(drecv.at[d - 1], d_r.at[d - 1])
        total = total + drecv[d - 1]
    lead_id = p * lrows + lax.broadcasted_iota(jnp.int32, (lrows, AB), 0)
    keep = jnp.where(lead_id < sn_ref[k], 1.0, 0.0) * col_live
    diag_ref[...] = (piv_ref[...] - total) * keep

    for cond, rem in zsends:
        @pl.when(cond)
        def _(rem=rem):
            rem.wait_send()
    for i in range(8):
        @pl.when(is_src)
        def _(i=i):
            for cp in x_src(i):
                cp.wait_send()

        @pl.when(jnp.logical_not(is_src))
        def _(i=i):
            x_mid(i)[3].wait_send()
    for m in range(MCH):
        for cp in a_own(m) + a_fwd(m) + a_opp(m):
            cp.wait_send()
        for j in range(1, 4):
            c_copy(m, j).wait_send()
    for cp in h_own + [h_fwd] + dcopies:
        cp.wait_send()


def per_device(ancestor_inverse, factor_panel, pivot_inverse, sn_size, anc_list):
    rows, cols = factor_panel.shape
    kw = ancestor_inverse.shape[1]
    lrows = pivot_inverse.shape[0]
    mrows = rows // MCH
    tiles = mrows // AB
    vm, dma = pltpu.VMEM, pltpu.SemaphoreType.DMA
    bf, f32 = jnp.bfloat16, jnp.float32
    vspec = pl.BlockSpec(memory_space=pltpu.VMEM)
    return pl.pallas_call(
        kernel,
        out_shape=(jax.ShapeDtypeStruct((cols, rows), bf),
                   jax.ShapeDtypeStruct((lrows, cols), f32)),
        in_specs=[pl.BlockSpec(memory_space=pl.ANY), vspec, vspec,
                  pl.BlockSpec(memory_space=pltpu.SMEM), vspec],
        out_specs=(vspec, vspec),
        scratch_shapes=[
            vm((4, rows, 2 * kw), bf),
            vm((rows, cols), bf),
            vm((4, 2 * kw, 4 * cols), bf),
            vm((rows, W), bf),
            vm((16, cols), f32),
            vm((mrows, 4 * cols), f32),
            vm((rows, cols), f32),
            vm((MCH, 3, tiles, AB + 16, cols), jnp.int16),
            vm((MCH, 3, tiles, AB + 16, cols), jnp.int16),
            vm((mrows, cols), bf),
            vm((W, cols), f32),
            vm((7, lrows, cols), f32),
            dma((MCH,)), dma((4,)), dma((16,)), dma((16,)),
            dma((MCH, 9)), dma((MCH, 4)), dma((MCH, 5)),
            dma((MCH, 3)), dma((MCH, 3)),
            dma((4,)), dma((3,)), dma((7,)), dma((7,)),
        ],
        compiler_params=pltpu.CompilerParams(
            collective_id=0, has_side_effects=True, vmem_limit_bytes=44 * 1024 * 1024),
        cost_estimate=pl.CostEstimate(flops=5_000_000_000, bytes_accessed=4_000_000, transcendentals=0),
    )(ancestor_inverse, factor_panel, pivot_inverse, sn_size, anc_list)


def solution(mesh):
    return jax.shard_map(
        per_device,
        mesh=mesh,
        in_specs=(P("prow", "pcol"), P("prow", "pcol"), P("prow", "pcol"), P(), P()),
        out_specs=(P("pcol", "prow"), P("prow", "pcol")),
        check_vma=False,
    )
```

time: 670 us -> 125 us (0.19)
  the two profiles are of different devices: /device:TPU:57 before, /device:TPU:112 now
where the time goes in v1:
time: 125 us
  Pallas kernels  119 us (95%)
  local copies, waits for them, and re-layouts  5.72 us (5%)
    pallas_call x1, Pallas kernels, per_device(): pl.pallas_call(kernel, out_shape=(jax.ShapeDtypeStruct((cols, rows), bf),...  119 us
    unnamed x12, local copies, waits for them, and re-layouts  5.72 us

profile of v1, /device:TPU:112, one launch (start us, length us, event | category | flops | bytes accessed | tf_op | source)
XLA Modules:
  0.0 125.1 jit_solution(6352802443666661564)
XLA Ops:
  0.6 0.0 copy-start
  0.6 1.3 %copy-done = bf16[1536,384]{1,0:T(8,128)(2,1)S(1)} copy-done((bf16[1536,384]{1,0:T(8,128)(2,1)S(1)}, bf16[1536,384]{1,0:T(8,128)(2,1)}, u32[]{:S(2)}) %copy-start) | copy-done | bytes 1179672
  1.9 0.0 copy-start.1
  1.9 1.0 copy-done.1
  2.9 0.0 copy-start.2
  2.9 0.8 copy-done.2
  3.7 0.0 copy-start.3
  3.7 0.7 copy-done.3
  4.3 0.0 copy-start.4
  4.3 0.7 copy-done.4
  5.0 118.7 %shard_map.68 = (bf16[128,1536]{1,0:T(8,128)(2,1)S(1)}, f32[64,128]{1,0:T(8,128)S(1)}) custom-call(bf16[1536,384]{1,0:T(8,128)(2,1)S(1)} %copy-done, bf16[1536,128]{1,0:T(8,128)(2,1)S(1)} %copy-done.1, f32[64,128]{1,0:T(8,128)S(1)} %copy-done.2, s32[8]{0:T(128)S(1)} %copy-done.4, s32[8,48]{1,0:T(8,128)S(1)} %copy-done.3), custom_call_target="tpu_custom_call" | custom-call | flops 5000000000 | bytes 4000000 | tf_op jit(solution)/shard_map/pallas_call | solution.py:327
  123.7 0.7 copy.9
  124.5 0.6 copy.10
Async XLA Ops:
  0.6 1.3 %copy-start = (bf16[1536,384]{1,0:T(8,128)(2,1)S(1)}, bf16[1536,384]{1,0:T(8,128)(2,1)}, u32[]{:S(2)}) copy-start(bf16[1536,384]{1,0:T(8,128)(2,1)} %a_ref.1) | copy-start | bytes 3538948
  1.9 1.0 copy-start.1
  2.9 0.8 copy-start.2
  3.7 0.7 copy-start.3
  4.3 0.7 copy-start.4

commit v2 on v1

v2 whole, which is shorter than its diff:
```python
import jax
import jax.numpy as jnp
from jax import lax
from jax.experimental import pallas as pl
from jax.experimental.pallas import tpu as pltpu
from jax.sharding import PartitionSpec as P

AB = 128
W = 512
MESH = pl.DeviceIdType.MESH
MCH = 4
JOF = (1, 3, 2, 0)
LANE = (3, 0, 2, 1)


def kernel(
    a_ref, l_ref, piv_ref, sn_ref, anc_ref, out_ref, diag_ref,
    abuf, l_in, piv, anc, lhat, spread, lbuf, lead, live, acc, cown, csend, crecv, abf, corr, drecv,
    ld_sem, in_sem, s1_s, s1_r, s2_s, s2_r, s3_s, s3_r, a_s, a_r, ab_r, c_s, c_r, h_s, h_r, d_s, d_r,
):
    rows = l_ref.shape[0]
    mrows = rows // MCH
    half = rows // 2
    quart = half // 4
    kw = a_ref.shape[1]
    tiles = mrows // AB
    p = lax.axis_index("prow")
    q = lax.axis_index("pcol")
    x, zh = p % 4, p // 4
    y, zl, c = q // 8, (q // 2) % 4, q % 2
    z = zh * 4 + zl
    k = q // 4

    def dev(x_, y_, z_, c_):
        return ((z_ // 4) * 4 + x_, y_ * 8 + (z_ % 4) * 2 + c_)

    def at_x(d):
        return dev((x + d) % 4, y, z, c)

    def at_y(d):
        return dev(x, (y + d) % 4, z, c)

    def at_z(z_):
        return dev(x, y, z_, c)

    sib = dev(x, y, z, 1 - c)

    def rcopy(src, dst, ssem, rsem, device):
        return pltpu.make_async_remote_copy(
            src_ref=src, dst_ref=dst, send_sem=ssem, recv_sem=rsem,
            device_id=device, device_id_type=MESH)

    barrier = pltpu.get_barrier_semaphore()
    partners = [at_z((z + d) % 8) for d in range(1, 8)]
    partners += [dev((x + d) % 4, y, ((zh + e) % 2) * 4 + zl, c)
                 for d in range(1, 4) for e in range(2)]
    partners += [at_y(1), at_y(3), sib]
    for partner in partners:
        pl.semaphore_signal(barrier, inc=1, device_id=partner, device_id_type=MESH)

    def mchunk(m):
        return pl.ds(m * mrows, mrows)

    def ablk(y_, c_, r):
        return abuf.at[y_, r, pl.ds(pl.multiple_of(c_ * kw, 128), kw)]

    def load(m):
        r = mchunk(m)
        return pltpu.make_async_copy(a_ref.at[r, :], ablk(y, c, r), ld_sem.at[m])

    l_load = pltpu.make_async_copy(l_ref, l_in, in_sem.at[0])
    anc_load = pltpu.make_async_copy(anc_ref, anc, in_sem.at[1])
    piv_load = pltpu.make_async_copy(piv_ref, piv, in_sem.at[2])
    l_load.start()
    anc_load.start()
    for m in range(MCH):
        load(m).start()
    piv_load.start()

    l_load.wait()
    anc_load.wait()
    ids = p * (rows // AB) + lax.broadcasted_iota(jnp.int32, (16, anc_ref.shape[1]), 0)
    hit = jnp.where(ids == anc[pl.ds(k, 1), :], 1.0, 0.0)
    row_live = jnp.max(hit, axis=1, keepdims=True)
    cols = (q % 4) * AB + lax.broadcasted_iota(jnp.int32, (1, AB), 1)
    col_live = jnp.where(cols < sn_ref[k], 1.0, 0.0)
    live[...] = row_live * col_live
    for b in range(rows // AB):
        r = pl.ds(b * AB, AB)
        lhat[r, :] = (l_in[r, :].astype(jnp.float32) * live[b:b + 1, :]).astype(jnp.bfloat16)
    for h in range(2):
        mine = pl.ds(pl.multiple_of(h * half + x * quart, 64), quart)
        spread[x % 2, h, x // 2] = lhat[mine, :]

    pl.semaphore_wait(barrier, len(partners))

    def s1(d, h):
        s = (x + d) % 4
        return rcopy(lhat.at[pl.ds(pl.multiple_of(h * half + s * quart, 64), quart), :],
                     spread.at[x % 2, h, x // 2], s1_s.at[d - 1, h], s1_r.at[d - 1, h], at_x(d))

    for d in (1, 3, 2):
        for h in range(2):
            s1(d, h).start()

    def a_own(m):
        r = mchunk(m)
        blk = ablk(y, c, r)
        return [rcopy(blk, blk, a_s.at[m, 0], a_r.at[m, 0], at_y(1)),
                rcopy(blk, blk, a_s.at[m, 1], a_r.at[m, 1], at_y(3)),
                rcopy(blk, blk, a_s.at[m, 2], ab_r.at[m, 0], sib)]

    hr = mrows // 2
    ym, yp, yo = (y + 3) % 4, (y + 1) % 4, (y + 2) % 4

    def a_fwd(m):
        lo, hi = pl.ds(m * mrows, hr), pl.ds(m * mrows + hr, hr)
        r = mchunk(m)
        return [rcopy(ablk(ym, c, lo), ablk(ym, c, lo), a_s.at[m, 3], a_r.at[m, 2], at_y(1)),
                rcopy(ablk(yp, c, hi), ablk(yp, c, hi), a_s.at[m, 4], a_r.at[m, 3], at_y(3)),
                rcopy(ablk(ym, c, r), ablk(ym, c, r), a_s.at[m, 5], ab_r.at[m, 1], sib),
                rcopy(ablk(yp, c, r), ablk(yp, c, r), a_s.at[m, 6], ab_r.at[m, 2], sib)]

    def a_opp(m):
        lo, hi = pl.ds(m * mrows, hr), pl.ds(m * mrows + hr, hr)
        return [rcopy(ablk(yo, c, lo), ablk(yo, c, lo), a_s.at[m, 7], ab_r.at[m, 3], sib),
                rcopy(ablk(yo, c, hi), ablk(yo, c, hi), a_s.at[m, 8], ab_r.at[m, 4], sib)]

    def wait_into(ref, sem):
        pltpu.make_async_copy(ref, ref, sem).wait()

    def own_send(m):
        load(m).wait()
        for cp in a_own(m):
            cp.start()

    def relay_a(m):
        r = mchunk(m)
        cps = a_fwd(m)
        wait_into(ablk(ym, c, r), a_r.at[m, 0])
        cps[0].start()
        cps[2].start()
        wait_into(ablk(yp, c, r), a_r.at[m, 1])
        cps[1].start()
        cps[3].start()

    def finish_a(m):
        r = mchunk(m)
        lo, hi = pl.ds(m * mrows, hr), pl.ds(m * mrows + hr, hr)
        cps = a_opp(m)
        wait_into(ablk(yo, c, lo), a_r.at[m, 2])
        cps[0].start()
        wait_into(ablk(yo, c, hi), a_r.at[m, 3])
        cps[1].start()

    def wait_a(m):
        r = mchunk(m)
        lo, hi = pl.ds(m * mrows, hr), pl.ds(m * mrows + hr, hr)
        oc = 1 - c
        wait_into(ablk(y, oc, r), ab_r.at[m, 0])
        wait_into(ablk(ym, oc, r), ab_r.at[m, 1])
        wait_into(ablk(yp, oc, r), ab_r.at[m, 2])
        wait_into(ablk(yo, oc, lo), ab_r.at[m, 3])
        wait_into(ablk(yo, oc, hi), ab_r.at[m, 4])

    own_send(0)
    own_send(1)

    def lanes(d):
        return pl.ds(LANE[d % 4] * AB, AB)

    def s2(d):
        tz = ((z + d) % 8) % 4
        src = spread.at[tz // 2, tz % 2]
        dst = lbuf.at[pl.ds(zh * 2, 2), pl.ds(pl.multiple_of(x * quart, 64), quart), lanes(8 - d)]
        if d == 0:
            return pltpu.make_async_copy(src, dst, s2_r.at[0])
        return rcopy(src, dst, s2_s.at[d], s2_r.at[(8 - d) % 8], at_z((z + d) % 8))

    for h in range(2):
        for d in (1, 3, 2):
            xf = (x + 4 - d) % 4
            wait_into(spread.at[xf % 2, h, xf // 2], s1_r.at[d - 1, h])
    for d in (7, 3, 1, 5, 6, 2, 4, 0):
        s2(d).start()

    def piece(d, s):
        zs = (z + d) % 8
        return lbuf.at[pl.ds((zs // 4) * 2, 2), pl.ds(pl.multiple_of(s * quart, 64), quart), lanes(d)]

    def piece1(d, s, xs):
        zs = (z + d) % 8
        return lbuf.at[(zs // 4) * 2 + xs, pl.ds(pl.multiple_of(s * quart, 64), quart), lanes(d)]

    xm, xp, xo = (x + 3) % 4, (x + 1) % 4, (x + 2) % 4

    def s3(d):
        return [rcopy(piece(d, x), piece(d, x), s3_s.at[d, 0], s3_r.at[d, 0], at_x(1)),
                rcopy(piece(d, x), piece(d, x), s3_s.at[d, 1], s3_r.at[d, 1], at_x(3))]

    def s3_relay(d):
        return [rcopy(piece1(d, xm, 0), piece1(d, xm, 0), s3_s.at[d, 2], s3_r.at[d, 2], at_x(1)),
                rcopy(piece1(d, xp, 1), piece1(d, xp, 1), s3_s.at[d, 3], s3_r.at[d, 3], at_x(3))]

    GROUPS = ((1, 5), (7, 3), (2, 6), (0, 4))

    def spread_x(g):
        for d in GROUPS[g]:
            wait_into(piece(d, x), s2_r.at[d])
            for cp in s3(d):
                cp.start()

    def relay_x(g):
        for d in GROUPS[g]:
            cps = s3_relay(d)
            wait_into(piece(d, xm), s3_r.at[d, 0])
            cps[0].start()
            wait_into(piece(d, xp), s3_r.at[d, 1])
            cps[1].start()

    def wait_x(g):
        for d in GROUPS[g]:
            wait_into(piece1(d, xo, 0), s3_r.at[d, 2])
            wait_into(piece1(d, xo, 1), s3_r.at[d, 3])

    zmate = z + 1 - 2 * (z % 2)

    def hblk(zb, cb):
        return lead.at[:, pl.ds(pl.multiple_of(((zb % 2) * 2 + cb) * AB, 128), AB)]

    h_own = [rcopy(lhat, hblk(z, c), h_s.at[0], h_r.at[0], at_z(zmate)),
             rcopy(lhat, hblk(z, c), h_s.at[1], h_r.at[1], sib)]
    h_fwd = rcopy(hblk(zmate, c), hblk(zmate, c), h_s.at[2], h_r.at[2], sib)
    h_loc = pltpu.make_async_copy(lhat, hblk(z, c), h_s.at[3])

    def c_copy(m, n):
        return rcopy(csend.at[m, n], crecv.at[m, n], c_s.at[m, n], c_r.at[m, n],
                     at_z(zh * 4 + (zl + JOF[n]) % 4))

    def compute(m, n0, n1):
        r = mchunk(m)
        ln = pl.ds(n0 * AB, (n1 - n0) * AB)
        acc[:, ln] = jnp.dot(abuf[0, r, :], lbuf[0, :, ln], preferred_element_type=jnp.float32)
        for yy in range(1, 4):
            acc[:, ln] += jnp.dot(abuf[yy, r, :], lbuf[yy, :, ln], preferred_element_type=jnp.float32)
        for n in range(n0, n1):
            if JOF[n] == 0:
                cown[r, :] = acc[:, n * AB:(n + 1) * AB]
                continue
            for t in range(tiles):
                part = acc[t * AB:(t + 1) * AB, n * AB:(n + 1) * AB]
                top = jnp.max(jnp.abs(part), axis=0, keepdims=True)
                e = jnp.clip(jnp.floor(jnp.log2(jnp.maximum(top, 1e-30))) + 1.0, -90.0, 90.0)
                v = jnp.clip(jnp.round(part * jnp.exp2(15.0 - e)), -32767.0, 32767.0)
                csend[m, n, t, 0:AB, :] = v.astype(jnp.int32).astype(jnp.int16)
                csend[m, n, t, AB:AB + 16, :] = jnp.broadcast_to(
                    e.astype(jnp.int32), (16, AB)).astype(jnp.int16)
            c_copy(m, n).start()

    spread_x(0)
    relay_a(0)
    own_send(2)
    spread_x(1)
    relay_x(0)
    spread_x(2)
    relay_x(1)
    finish_a(0)
    relay_a(1)
    own_send(3)
    spread_x(3)
    h_loc.start()
    for cp in h_own:
        cp.start()
    relay_x(2)
    wait_x(0)
    wait_x(1)
    wait_a(0)
    compute(0, 0, 2)
    relay_x(3)
    finish_a(1)
    wait_a(1)
    compute(1, 0, 2)
    relay_a(2)
    wait_x(2)
    wait_x(3)
    compute(0, 2, 4)
    compute(1, 2, 4)
    relay_a(3)
    finish_a(2)
    wait_a(2)
    compute(2, 0, 4)
    wait_into(hblk(zmate, c), h_r.at[0])
    h_fwd.start()
    finish_a(3)
    wait_a(3)
    compute(3, 0, 4)
    h_loc.wait()
    wait_into(hblk(z, 1 - c), h_r.at[1])
    wait_into(hblk(zmate, 1 - c), h_r.at[2])

    for m in range(MCH):
        for n in range(3):
            wait_into(crecv.at[m, n], c_r.at[m, n])
        for t in range(tiles):
            at = m * mrows + t * AB
            s = cown[at:at + AB, :]
            for n in range(3):
                v = crecv[m, n, t, 0:AB, :].astype(jnp.int32).astype(jnp.float32)
                e = crecv[m, n, t, AB:AB + 16, :].astype(jnp.int32).astype(jnp.float32)
                s = s + v * jnp.exp2(e[0:1, :] - 15.0)
            b = m * tiles + t
            s = -(s * live[b:b + 1, :])
            abf[t * AB:(t + 1) * AB, :] = s.astype(jnp.bfloat16)
            out_ref[:, at:at + AB] = s.T.astype(jnp.bfloat16)
        part = lax.dot_general(
            lead[mchunk(m), :], abf[...], (((0,), (0,)), ((), ())), preferred_element_type=jnp.float32)
        corr[...] = part if m == 0 else corr[...] + part

    lrows = diag_ref.shape[0]

    def mine(p_):
        return pl.ds(pl.multiple_of(p_ * lrows, lrows), lrows)

    dcopies = []
    for d in range(1, 8):
        to = (p + d) % 8
        cp = rcopy(corr.at[mine(to), :], drecv.at[d - 1], d_s.at[d - 1], d_r.at[d - 1], (to, q))
        cp.start()
        dcopies.append(cp)
    total = corr[mine(p), :]
    for d in range(1, 8):
        wait_into(drecv.at[d - 1], d_r.at[d - 1])
        total = total + drecv[d - 1]
    lead_id = p * lrows + lax.broadcasted_iota(jnp.int32, (lrows, AB), 0)
    keep = jnp.where(lead_id < sn_ref[k], 1.0, 0.0) * col_live
    piv_load.wait()
    diag_ref[...] = (piv[...] - total) * keep

    for d in range(1, 4):
        for h in range(2):
            s1(d, h).wait_send()
    for d in range(8):
        if d:
            s2(d).wait_send()
        for cp in s3(d) + s3_relay(d):
            cp.wait_send()
    for m in range(MCH):
        for cp in a_own(m) + a_fwd(m) + a_opp(m):
            cp.wait_send()
        for n in range(3):
            c_copy(m, n).wait_send()
    for cp in h_own + [h_fwd] + dcopies:
        cp.wait_send()


def per_device(ancestor_inverse, factor_panel, pivot_inverse, sn_size, anc_list):
    rows, cols = factor_panel.shape
    kw = ancestor_inverse.shape[1]
    lrows = pivot_inverse.shape[0]
    mrows = rows // MCH
    tiles = mrows // AB
    vm, dma = pltpu.VMEM, pltpu.SemaphoreType.DMA
    bf, f32 = jnp.bfloat16, jnp.float32
    anys = pl.BlockSpec(memory_space=pl.ANY)
    vspec = pl.BlockSpec(memory_space=pltpu.VMEM)
    return pl.pallas_call(
        kernel,
        out_shape=(jax.ShapeDtypeStruct((cols, rows), bf),
                   jax.ShapeDtypeStruct((lrows, cols), f32)),
        in_specs=[anys, anys, anys, pl.BlockSpec(memory_space=pltpu.SMEM), anys],
        out_specs=(vspec, vspec),
        scratch_shapes=[
            vm((4, rows, 2 * kw), bf),
            vm((rows, cols), bf),
            vm((lrows, cols), f32),
            vm(anc_list.shape, jnp.int32),
            vm((rows, cols), bf),
            vm((2, 2, 2, rows // 8, cols), bf),
            vm((4, 2 * kw, 4 * cols), bf),
            vm((rows, W), bf),
            vm((16, cols), f32),
            vm((mrows, 4 * cols), f32),
            vm((rows, cols), f32),
            vm((MCH, 3, tiles, AB + 16, cols), jnp.int16),
            vm((MCH, 3, tiles, AB + 16, cols), jnp.int16),
            vm((mrows, cols), bf),
            vm((W, cols), f32),
            vm((7, lrows, cols), f32),
            dma((MCH,)), dma((3,)), dma((3, 2)), dma((3, 2)),
            dma((8,)), dma((8,)), dma((8, 4)), dma((8, 4)),
            dma((MCH, 9)), dma((MCH, 4)), dma((MCH, 5)),
            dma((MCH, 3)), dma((MCH, 3)),
            dma((4,)), dma((3,)), dma((7,)), dma((7,)),
        ],
        compiler_params=pltpu.CompilerParams(
            collective_id=0, has_side_effects=True, vmem_limit_bytes=60 * 1024 * 1024),
        cost_estimate=pl.CostEstimate(flops=5_000_000_000, bytes_accessed=4_000_000, transcendentals=0),
    )(ancestor_inverse, factor_panel, pivot_inverse, sn_size, anc_list)


def solution(mesh):
    return jax.shard_map(
        per_device,
        mesh=mesh,
        in_specs=(P("prow", "pcol"), P("prow", "pcol"), P("prow", "pcol"), P(), P()),
        out_specs=(P("pcol", "prow"), P("prow", "pcol")),
        check_vma=False,
    )
```

time: 125 us -> 102 us (0.82)
  the two profiles are of different devices: /device:TPU:112 before, /device:TPU:22 now
where the time goes in v2:
time: 102 us; the launch traced here: 101 us
  Pallas kernels  97.6 us (96%)
  local copies, waits for them, and re-layouts  3.14 us (3%)
    pallas_call x1, Pallas kernels, per_device(): pl.pallas_call(kernel, out_shape=(jax.ShapeDtypeStruct((cols, rows), bf),...  97.6 us
    unnamed x2, local copies, waits for them, and re-layouts  3.14 us

profile of v2, /device:TPU:22, one launch (start us, length us, event | category | flops | bytes accessed | tf_op | source)
XLA Modules:
  0.0 101.4 jit_solution(1565655429846534372)
XLA Ops:
  0.6 97.6 %shard_map.68 = (bf16[128,1536]{1,0:T(8,128)(2,1)}, f32[64,128]{1,0:T(8,128)}) custom-call(bf16[1536,384]{1,0:T(8,128)(2,1)} %a_ref.1, bf16[1536,128]{1,0:T(8,128)(2,1)} %l_ref.1, f32[64,128]{1,0:T(8,128)} %piv_ref.1, s32[8]{0:T(128)} %sn_ref.1, s32[8,48]{1,0:T(8,128)} %anc_ref.1), custom_call_target="tpu_custom_call" | custom-call | flops 5000000000 | bytes 4000000 | tf_op jit(solution)/shard_map/pallas_call | solution.py:366
  98.2 1.8 %copy.9 = bf16[128,1536]{1,0:T(8,128)(2,1)} copy(bf16[128,1536]{1,0:T(8,128)(2,1)} %get-tuple-element.4) | data formatting | bytes 786432
  100.0 1.4 %copy.10 = f32[64,128]{1,0:T(8,128)} copy(f32[64,128]{1,0:T(8,128)} %get-tuple-element.5) | data formatting | bytes 65536

commit v3 on v2

v3 whole, which is shorter than its diff:
```python
import jax
import jax.numpy as jnp
from jax import lax
from jax.experimental import pallas as pl
from jax.experimental.pallas import tpu as pltpu
from jax.sharding import PartitionSpec as P

AB = 128
W = 512
MESH = pl.DeviceIdType.MESH
CHUNKS = (3, 3, 3, 2, 1)
MCH = len(CHUNKS)
TOP = max(CHUNKS)
JOF = (1, 3, 2, 0)
LANE = (3, 0, 2, 1)


def kernel(
    a_ref, l_ref, piv_ref, sn_ref, anc_ref, out_ref, diag_ref,
    abuf, l_in, piv, anc, lhat, away, lbuf, lead, live, acc, cown, csend, crecv, ckeep, tot, abf, corr, dsend, drecv, out_v, diag_v,
    in_sem, s_s, x_r, s2_r, s3_r, a_r, ab_r, c_r, h_r, out_s,
):
    rows = l_ref.shape[0]
    half = rows // 2
    quart = half // 4
    kw = a_ref.shape[1]
    first = [sum(CHUNKS[:m]) * AB for m in range(MCH)]
    p = lax.axis_index("prow")
    q = lax.axis_index("pcol")
    x, zh = p % 4, p // 4
    y, zl, c = q // 8, (q // 2) % 4, q % 2
    z = zh * 4 + zl
    k = q // 4

    def dev(x_, y_, z_, c_):
        return ((z_ // 4) * 4 + x_, y_ * 8 + (z_ % 4) * 2 + c_)

    def at_x(d):
        return dev((x + d) % 4, y, z, c)

    def at_y(d):
        return dev(x, (y + d) % 4, z, c)

    def at_z(z_):
        return dev(x, y, z_, c)

    sib = dev(x, y, z, 1 - c)

    def rcopy(src, dst, ssem, rsem, device):
        return pltpu.make_async_remote_copy(
            src_ref=src, dst_ref=dst, send_sem=ssem, recv_sem=rsem,
            device_id=device, device_id_type=MESH)

    barrier = pltpu.get_barrier_semaphore()
    partners = [at_z((z + d) % 8) for d in range(1, 8)]
    partners += [dev((x + d) % 4, y, ((zh + e) % 2) * 4 + zl, c)
                 for d in range(1, 4) for e in range(2)]
    partners += [at_y(1), at_y(3), sib]
    for partner in partners:
        pl.semaphore_signal(barrier, inc=1, device_id=partner, device_id_type=MESH)

    def mchunk(m):
        return pl.ds(first[m], CHUNKS[m] * AB)

    def mhalves(m):
        n = CHUNKS[m] * AB // 2
        return pl.ds(first[m], n), pl.ds(first[m] + n, n)

    def ablk(y_, c_, r):
        return abuf.at[y_, r, pl.ds(pl.multiple_of(c_ * kw, 128), kw)]

    a_load = pltpu.make_async_copy(a_ref, ablk(y, c, pl.ds(0, rows)), in_sem.at[3])
    l_load = pltpu.make_async_copy(l_ref, l_in, in_sem.at[0])
    anc_load = pltpu.make_async_copy(anc_ref, anc, in_sem.at[1])
    piv_load = pltpu.make_async_copy(piv_ref, piv, in_sem.at[2])
    l_load.start()
    anc_load.start()
    a_load.start()
    piv_load.start()

    l_load.wait()
    anc_load.wait()
    ids = p * (rows // AB) + lax.broadcasted_iota(jnp.int32, (16, anc_ref.shape[1]), 0)
    hit = jnp.where(ids == anc[pl.ds(k, 1), :], 1.0, 0.0)
    row_live = jnp.max(hit, axis=1, keepdims=True)
    cols = (q % 4) * AB + lax.broadcasted_iota(jnp.int32, (1, AB), 1)
    col_live = jnp.where(cols < sn_ref[k], 1.0, 0.0)
    live[...] = row_live * col_live
    for b in range(rows // AB):
        r = pl.ds(b * AB, AB)
        w = (l_in[r, :].astype(jnp.float32) * live[b:b + 1, :]).astype(jnp.bfloat16)
        lhat[b * AB // half, pl.ds(b * AB % half, AB), :] = w

    pl.semaphore_wait(barrier, len(partners))

    s1 = [rcopy(lhat.at[:, pl.ds((2 + i) * quart, quart), :], away.at[i], s_s.at[0], x_r.at[0], at_x(1 + 2 * i))
          for i in range(2)]
    for cp in s1:
        cp.start()

    def lanes(d):
        return pl.ds(LANE[d % 4] * AB, AB)

    def place(x_, zl_, zh_, i):
        home = 1 - (x_ + zl_ // 2) % 2
        xs = home * (x_ // 2) + (1 - home) * (((x_ + 3 + 2 * i) % 4) // 2)
        row = (1 - home) * 2 * quart + i * quart
        return zh_ * 2 + xs, pl.ds(pl.multiple_of(row, 64), quart)

    def s2(d, i, home):
        tz = (z + d) % 4
        src = lhat.at[tz % 2, pl.ds(i * quart, quart), :] if home else away.at[i, tz % 2]
        blk, row = place(x, tz, zh, i)
        dst = lbuf.at[blk, row, lanes(8 - d)]
        sem = s2_r.at[(8 - d) % 8]
        if d == 0:
            return pltpu.make_async_copy(src, dst, sem)
        return rcopy(src, dst, s_s.at[1], sem, at_z((z + d) % 8))

    S2_ORDER = ((7, 3), (1, 5), (6, 2), (4, 0))
    homes = [1 - (x + ((z + g[0]) % 4) // 2) % 2 for g in S2_ORDER]
    first_home = [homes[0], (1 - homes[0]) * homes[1], (1 - homes[0]) * (1 - homes[1]), 0]
    first_away = [1 - homes[0], homes[0] * (1 - homes[1]), homes[0] * homes[1], 0]

    def s2_start(when, home):
        for g, cond in zip(S2_ORDER, when):
            @pl.when(cond == 1)
            def _(g=g):
                for d in g:
                    for i in range(2):
                        s2(d, i, home).start()

    s2_start(first_home, True)

    zmate = z + 1 - 2 * (z % 2)

    def hblk(zb, cb):
        return lead.at[:, :, pl.ds(pl.multiple_of(((zb % 2) * 2 + cb) * AB, 128), AB)]

    h_own = [rcopy(lhat, hblk(z, c), s_s.at[4], h_r.at[0], at_z(zmate)),
             rcopy(lhat, hblk(z, c), s_s.at[4], h_r.at[1], sib)]
    h_fwd = rcopy(hblk(zmate, c), hblk(zmate, c), s_s.at[4], h_r.at[1], sib)
    h_loc = pltpu.make_async_copy(lhat, hblk(z, c), h_r.at[2])

    def send_lead():
        h_loc.start()
        for cp in h_own:
            cp.start()

    def a_own(m):
        r = mchunk(m)
        blk = ablk(y, c, r)
        return [rcopy(blk, blk, s_s.at[3], a_r.at[m, 0], at_y(1)),
                rcopy(blk, blk, s_s.at[3], a_r.at[m, 0], at_y(3)),
                rcopy(blk, blk, s_s.at[3], ab_r.at[m], sib)]

    ym, yp, yo = (y + 3) % 4, (y + 1) % 4, (y + 2) % 4

    def a_fwd(m):
        lo, hi = mhalves(m)
        r = mchunk(m)
        return [rcopy(ablk(ym, c, lo), ablk(ym, c, lo), s_s.at[3], a_r.at[m, 1], at_y(1)),
                rcopy(ablk(yp, c, hi), ablk(yp, c, hi), s_s.at[3], a_r.at[m, 1], at_y(3)),
                rcopy(ablk(ym, c, r), ablk(ym, c, r), s_s.at[3], ab_r.at[m], sib),
                rcopy(ablk(yp, c, r), ablk(yp, c, r), s_s.at[3], ab_r.at[m], sib)]

    def a_opp(m):
        r = mchunk(m)
        return [rcopy(ablk(yo, c, r), ablk(yo, c, r), s_s.at[3], ab_r.at[m], sib)]

    def wait_into(ref, sem):
        pltpu.make_async_copy(ref, ref, sem).wait()

    def own_send(m):
        for cp in a_own(m):
            cp.start()

    def relay_a(m):
        wait_into(abuf.at[pl.ds(0, 2), mchunk(m), pl.ds(0, kw)], a_r.at[m, 0])
        for cp in a_fwd(m):
            cp.start()

    def finish_a(m):
        wait_into(abuf.at[0, mchunk(m), pl.ds(0, kw)], a_r.at[m, 1])
        for cp in a_opp(m):
            cp.start()

    def wait_a(m):
        wait_into(abuf.at[:, mchunk(m), pl.ds(0, kw)], ab_r.at[m])

    a_load.wait()
    own_send(0)
    own_send(1)
    own_send(2)

    wait_into(away, x_r.at[0])
    s2_start(first_away, False)
    s2_start([h - f for h, f in zip(homes, first_home)], True)
    s2_start([1 - h - f for h, f in zip(homes, first_away)], False)

    def piece(d, x_, i):
        blk, row = place(x_, zl, ((z + d) % 8) // 4, i)
        return lbuf.at[blk, row, lanes(d)]

    xm, xp, xo = (x + 3) % 4, (x + 1) % 4, (x + 2) % 4

    def s3(d, i):
        return [rcopy(piece(d, x, i), piece(d, x, i), s_s.at[2], s3_r.at[d, 0], at_x(1)),
                rcopy(piece(d, x, i), piece(d, x, i), s_s.at[2], s3_r.at[d, 1], at_x(3))]

    def s3_relay(d):
        return [rcopy(piece(d, xm, 0), piece(d, xm, 0), s_s.at[2], s3_r.at[d, 2], at_x(1)),
                rcopy(piece(d, xp, 1), piece(d, xp, 1), s_s.at[2], s3_r.at[d, 2], at_x(3))]

    GROUPS = ((1, 5), (7, 3), (2, 6), (0, 4))

    def wait_pair(sem):
        wait_into(lbuf.at[pl.ds(0, 2), pl.ds(0, quart), pl.ds(0, AB)], sem)

    def spread_x(g):
        for d in GROUPS[g]:
            wait_pair(s2_r.at[d])
            for i in range(2):
                for cp in s3(d, i):
                    cp.start()

    def relay_x(g):
        for d in GROUPS[g]:
            cps = s3_relay(d)
            wait_pair(s3_r.at[d, 0])
            cps[0].start()
            wait_pair(s3_r.at[d, 1])
            cps[1].start()

    def wait_x(g):
        for d in GROUPS[g]:
            wait_pair(s3_r.at[d, 2])

    is_end = zl * (3 - zl) == 0
    at_hi, at_lo = (zl + 1) // 4, (4 - zl) // 4

    def cout(m, n):
        return csend.at[n, pl.ds(first[m] + 16 * m, 16 + CHUNKS[m] * AB)]

    def c_copy(m, n):
        if n == 0:
            to, slot = zl + 1 - 2 * at_hi, 3 * at_hi
        elif n == 1:
            to, slot = zl - 1 + 2 * at_lo, 1 + 2 * at_lo
        else:
            to, slot = (zl + 2) % 4, 2
        t = pl.ds(0, 16 + CHUNKS[m] * AB)
        return rcopy(cout(m, n), crecv.at[m, slot, t], s_s.at[5], c_r.at[m, slot], at_z(zh * 4 + to))

    def code(part, dst, step=AB):
        n = part.shape[0]
        at = lax.broadcasted_iota(jnp.int32, (16, AB), 0)
        powers = jnp.zeros((16, AB), jnp.float32)
        for t in range(n // step):
            b = part[t * step:(t + 1) * step, :]
            top = jnp.max(jnp.abs(b), axis=0, keepdims=True)
            e = jnp.clip(jnp.floor(jnp.log2(jnp.maximum(top, 1e-30))) + 1.0, -90.0, 90.0)
            v = jnp.clip(jnp.round(b * jnp.exp2(15.0 - e)), -32767.0, 32767.0)
            dst[16 + t * step:16 + (t + 1) * step, :] = v.astype(jnp.int32).astype(jnp.int16)
            powers = jnp.where(at == t, e, powers)
        dst[0:16, :] = powers.astype(jnp.int32).astype(jnp.int16)

    def decode(src, t=0, step=AB):
        v = src[16 + t * step:16 + (t + 1) * step, :].astype(jnp.int32).astype(jnp.float32)
        e = src[0:16, :].astype(jnp.int32).astype(jnp.float32)
        return v * jnp.exp2(e[t:t + 1, :] - 15.0)

    def compute(m, n0, n1):
        r = mchunk(m)
        n = CHUNKS[m] * AB
        ln = pl.ds(n0 * AB, (n1 - n0) * AB)
        acc[0:n, ln] = jnp.dot(abuf[0, r, :], lbuf[0, :, ln], preferred_element_type=jnp.float32)
        for yy in range(1, 4):
            acc[0:n, ln] += jnp.dot(abuf[yy, r, :], lbuf[yy, :, ln], preferred_element_type=jnp.float32)
        for b in range(n0, n1):
            part = acc[0:n, b * AB:(b + 1) * AB]
            if b == 3:
                cown[r, :] = part
            elif b == 2:
                ckeep[m, 0:n, :] = part
                pl.when(is_end)(lambda: send_far(m))
            else:
                code(part, cout(m, b))
                c_copy(m, b).start()

    def send_far(m):
        code(ckeep[m, 0:CHUNKS[m] * AB, :], cout(m, 2))
        c_copy(m, 2).start()

    def wait_c(m, slot):
        wait_into(crecv.at[m, slot, pl.ds(0, 16 + CHUNKS[m] * AB)], c_r.at[m, slot])

    def merge(m):
        @pl.when(jnp.logical_not(is_end))
        def _():
            wait_c(m, 3)
            for t in range(CHUNKS[m]):
                ckeep[m, t * AB:(t + 1) * AB, :] += decode(crecv.at[m, 3], t)
            code(ckeep[m, 0:CHUNKS[m] * AB, :], cout(m, 2))
            c_copy(m, 2).start()

    def add_slot(m, n):
        wait_c(m, n)
        for t in range(CHUNKS[m]):
            tot[t * AB:(t + 1) * AB, :] += decode(crecv.at[m, n], t)

    def out_copy(m):
        return pltpu.make_async_copy(out_v.at[:, mchunk(m)], out_ref.at[:, mchunk(m)], out_s.at[0])

    def finish_c(m):
        n = CHUNKS[m] * AB
        tot[0:n, :] = cown[mchunk(m), :]
        pl.when(zl >= 1)(lambda: add_slot(m, 0))
        pl.when(zl <= 2)(lambda: add_slot(m, 1))
        add_slot(m, 2)
        for t in range(CHUNKS[m]):
            at = first[m] + t * AB
            b = at // AB
            v = -(tot[t * AB:(t + 1) * AB, :] * live[b:b + 1, :])
            abf[t * AB:(t + 1) * AB, :] = v.astype(jnp.bfloat16)
            out_v[:, at:at + AB] = v.T.astype(jnp.bfloat16)
        out_copy(m).start()
        part = lax.dot_general(
            lead[first[m] // half, pl.ds(first[m] % half, n), :], abf[0:n, :],
            (((0,), (0,)), ((), ())), preferred_element_type=jnp.float32)
        corr[...] = part if m == 0 else corr[...] + part

    def wait_lead():
        h_loc.wait()
        wait_into(lead.at[:, :, pl.ds(0, 2 * AB)], h_r.at[1])

    def fwd_lead():
        wait_into(hblk(zmate, c), h_r.at[0])
        h_fwd.start()

    def sent():
        wait_into(away, s_s.at[0])
        wait_into(abuf.at[0, pl.ds(0, 14 * quart * AB // (2 * kw)), :], s_s.at[1])
        wait_into(abuf.at[0], s_s.at[2])
        wait_into(abuf.at[:, pl.ds(0, rows * 7 // 8), :], s_s.at[3])
        wait_into(lead.at[:, :, pl.ds(0, 3 * AB)], s_s.at[4])

    spread_x(0)
    relay_a(0)
    spread_x(1)
    relay_x(0)
    relay_a(1)
    own_send(3)
    own_send(4)
    relay_x(1)
    spread_x(2)
    spread_x(3)
    send_lead()
    relay_a(2)
    finish_a(0)
    wait_x(0)
    wait_x(1)
    wait_a(0)
    compute(0, 0, 2)
    relay_x(2)
    finish_a(1)
    wait_a(1)
    compute(1, 0, 2)
    relay_x(3)
    relay_a(3)
    wait_x(2)
    wait_x(3)
    compute(0, 2, 4)
    relay_a(4)
    fwd_lead()
    compute(1, 2, 4)
    finish_a(2)
    merge(0)
    wait_a(2)
    compute(2, 0, 4)
    finish_a(3)
    merge(1)
    finish_a(4)
    wait_a(3)
    compute(3, 0, 4)
    wait_a(4)
    compute(4, 0, 4)
    wait_lead()
    merge(2)
    sent()
    finish_c(0)
    merge(3)
    finish_c(1)
    merge(4)
    finish_c(2)
    finish_c(3)
    finish_c(4)
    wait_into(csend, s_s.at[5])

    lrows = diag_ref.shape[0]

    def mine(p_):
        return pl.ds(pl.multiple_of(p_ * lrows, lrows), lrows)

    for d in (4, 1, 3, 2, 5, 7, 6):
        to = (zh + d // 4) % 2 * 4 + (x + d) % 4
        code(corr[mine(to), :], dsend.at[d - 1], lrows)
        cp = rcopy(dsend.at[d - 1], drecv.at[d - 1], s_s.at[6], x_r.at[1], (to, q))
        cp.start()
    total = corr[mine(p), :]
    wait_into(drecv, x_r.at[1])
    for d in range(1, 8):
        total = total + decode(drecv.at[d - 1], 0, lrows)
    lead_id = p * lrows + lax.broadcasted_iota(jnp.int32, (lrows, AB), 0)
    keep = jnp.where(lead_id < sn_ref[k], 1.0, 0.0) * col_live
    piv_load.wait()
    diag_v[...] = (piv[...] - total) * keep
    diag_copy = pltpu.make_async_copy(diag_v, diag_ref, out_s.at[1])
    diag_copy.start()
    wait_into(dsend, s_s.at[6])
    pltpu.make_async_copy(out_v, out_ref, out_s.at[0]).wait()
    diag_copy.wait()


def per_device(ancestor_inverse, factor_panel, pivot_inverse, sn_size, anc_list):
    rows, cols = factor_panel.shape
    kw = ancestor_inverse.shape[1]
    lrows = pivot_inverse.shape[0]
    vm, dma = pltpu.VMEM, pltpu.SemaphoreType.DMA
    bf, f32 = jnp.bfloat16, jnp.float32
    anys = pl.BlockSpec(memory_space=pl.ANY)
    return pl.pallas_call(
        kernel,
        out_shape=(jax.ShapeDtypeStruct((cols, rows), bf),
                   jax.ShapeDtypeStruct((lrows, cols), f32)),
        in_specs=[anys, anys, anys, pl.BlockSpec(memory_space=pltpu.SMEM), anys],
        out_specs=(anys, anys),
        scratch_shapes=[
            vm((4, rows, 2 * kw), bf),
            vm((rows, cols), bf),
            vm((lrows, cols), f32),
            vm(anc_list.shape, jnp.int32),
            vm((2, rows // 2, cols), bf),
            vm((2, 2, rows // 8, cols), bf),
            vm((4, 2 * kw, 4 * cols), bf),
            vm((2, rows // 2, W), bf),
            vm((16, cols), f32),
            vm((TOP * AB, 4 * cols), f32),
            vm((rows, cols), f32),
            vm((3, rows + 16 * MCH, cols), jnp.int16),
            vm((MCH, 4, 16 + TOP * AB, cols), jnp.int16),
            vm((MCH, TOP * AB, cols), f32),
            vm((TOP * AB, cols), f32),
            vm((TOP * AB, cols), bf),
            vm((W, cols), f32),
            vm((7, lrows + 16, cols), jnp.int16),
            vm((7, lrows + 16, cols), jnp.int16),
            vm((cols, rows), bf),
            vm((lrows, cols), f32),
            dma((4,)), dma((7,)), dma((2,)), dma((8,)), dma((8, 3)),
            dma((MCH, 2)), dma((MCH,)), dma((MCH, 4)), dma((3,)), dma((2,)),
        ],
        compiler_params=pltpu.CompilerParams(
            collective_id=0, has_side_effects=True, vmem_limit_bytes=60 * 1024 * 1024),
        cost_estimate=pl.CostEstimate(flops=5_000_000_000, bytes_accessed=4_000_000, transcendentals=0),
    )(ancestor_inverse, factor_panel, pivot_inverse, sn_size, anc_list)


def solution(mesh):
    return jax.shard_map(
        per_device,
        mesh=mesh,
        in_specs=(P("prow", "pcol"), P("prow", "pcol"), P("prow", "pcol"), P(), P()),
        out_specs=(P("pcol", "prow"), P("prow", "pcol")),
        check_vma=False,
    )
```

time: 102 us -> 92.6 us (0.908)
  the two profiles are of different devices: /device:TPU:22 before, /device:TPU:8 now
where the time goes in v3:
time: 92.6 us; the launch traced here: 92.4 us
  Pallas kernels  88.6 us (96%)
  local copies, waits for them, and re-layouts  3.14 us (3%)
    pallas_call x1, Pallas kernels, per_device(): pl.pallas_call(kernel, out_shape=(jax.ShapeDtypeStruct((cols, rows), bf),...  88.6 us
    unnamed x2, local copies, waits for them, and re-layouts  3.14 us

profile of v3, /device:TPU:8, one launch (start us, length us, event | category | flops | bytes accessed | tf_op | source)
XLA Modules:
  0.0 92.4 jit_solution(7082655900257907508)
XLA Ops:
  0.6 88.6 %shard_map.68 = (bf16[128,1536]{1,0:T(8,128)(2,1)}, f32[64,128]{1,0:T(8,128)}) custom-call(bf16[1536,384]{1,0:T(8,128)(2,1)} %a_ref.1, bf16[1536,128]{1,0:T(8,128)(2,1)} %l_ref.1, f32[64,128]{1,0:T(8,128)} %piv_ref.1, s32[8]{0:T(128)} %sn_ref.1, s32[8,48]{1,0:T(8,128)} %anc_ref.1), custom_call_target="tpu_custom_call" | custom-call | flops 5000000000 | bytes 4000000 | tf_op jit(solution)/shard_map/pallas_call | solution.py:432
  89.2 1.8 %copy.9 = bf16[128,1536]{1,0:T(8,128)(2,1)} copy(bf16[128,1536]{1,0:T(8,128)(2,1)} %get-tuple-element.4) | data formatting | bytes 786432
  91.0 1.4 %copy.10 = f32[64,128]{1,0:T(8,128)} copy(f32[64,128]{1,0:T(8,128)} %get-tuple-element.5) | data formatting | bytes 65536

commit v4 on v3

--- a/solution.py
+++ b/solution.py
@@ -11,8 +11,20 @@
 CHUNKS = (3, 3, 3, 2, 1)
 MCH = len(CHUNKS)
 TOP = max(CHUNKS)
-JOF = (1, 3, 2, 0)
-LANE = (3, 0, 2, 1)
+
+FIRST = (
+    ("spread_x", 0), ("relay_a", 0), ("own_send", 2), ("spread_x", 1), ("relay_x", 0), ("send_lead",), ("relay_a", 1),
+    ("own_send", 3), ("own_send", 4), ("relay_x", 1), ("spread_x", 2), ("finish_a", 0), ("relay_a", 2),
+)
+REST = (
+    ("wait_x", 0), ("wait_x", 1), ("spread_x", 3), ("wait_a", 0), ("compute", 0, 0, 2), ("relay_x", 2), ("finish_a", 1),
+    ("wait_a", 1), ("compute", 1, 0, 2), ("merge", 0), ("relay_x", 3), ("relay_a", 3), ("relay_a", 4),
+    ("wait_x", 2), ("compute", 0, 2, 3), ("finish_a", 2), ("merge", 1), ("fwd_lead",),
+    ("wait_x", 3), ("wait_a", 2), ("compute", 2, 0, 4), ("finish_a", 3), ("finish_a", 4),
+    ("wait_a", 3), ("compute", 3, 0, 4), ("merge", 2), ("wait_a", 4), ("compute", 4, 0, 4), ("compute", 1, 2, 4), ("compute", 0, 3, 4),
+    ("wait_lead",), ("sent",), ("merge", 3), ("finish_c", 0), ("merge", 4),
+    ("finish_c", 1), ("finish_c", 2), ("finish_c", 3), ("finish_c", 4),
+)
 
 
 def kernel(
@@ -35,6 +47,8 @@
     def dev(x_, y_, z_, c_):
         return ((z_ // 4) * 4 + x_, y_ * 8 + (z_ % 4) * 2 + c_)
 
+    other = ((zl + 2) % 4, 3 - zl, zl + 1 - 2 * (zl % 2), zl)
+
     def at_x(d):
         return dev((x + d) % 4, y, z, c)
 
@@ -98,8 +112,8 @@
     for cp in s1:
         cp.start()
 
-    def lanes(d):
-        return pl.ds(LANE[d % 4] * AB, AB)
+    def lanes(n):
+        return pl.ds(n * AB, AB)
 
     def place(x_, zl_, zh_, i):
         home = 1 - (x_ + zl_ // 2) % 2
@@ -107,30 +121,29 @@
         row = (1 - home) * 2 * quart + i * quart
         return zh_ * 2 + xs, pl.ds(pl.multiple_of(row, 64), quart)
 
-    def s2(d, i, home):
-        tz = (z + d) % 4
+    def s2(n, e, i, home):
+        tz = other[n]
         src = lhat.at[tz % 2, pl.ds(i * quart, quart), :] if home else away.at[i, tz % 2]
         blk, row = place(x, tz, zh, i)
-        dst = lbuf.at[blk, row, lanes(8 - d)]
-        sem = s2_r.at[(8 - d) % 8]
-        if d == 0:
+        dst = lbuf.at[blk, row, lanes(n)]
+        sem = s2_r.at[2 * n + e]
+        if n == 3 and e == 0:
             return pltpu.make_async_copy(src, dst, sem)
-        return rcopy(src, dst, s_s.at[1], sem, at_z((z + d) % 8))
-
-    S2_ORDER = ((7, 3), (1, 5), (6, 2), (4, 0))
-    homes = [1 - (x + ((z + g[0]) % 4) // 2) % 2 for g in S2_ORDER]
-    first_home = [homes[0], (1 - homes[0]) * homes[1], (1 - homes[0]) * (1 - homes[1]), 0]
-    first_away = [1 - homes[0], homes[0] * (1 - homes[1]), homes[0] * homes[1], 0]
-
-    def s2_start(when, home):
-        for g, cond in zip(S2_ORDER, when):
-            @pl.when(cond == 1)
-            def _(g=g):
-                for d in g:
+        return rcopy(src, dst, s_s.at[1], sem, at_z((zh + e) % 2 * 4 + tz))
+
+    is_home = (x + zl // 2) % 2 == 0
+    is_away = (x + zl // 2) % 2 == 1
+
+    def s2_start(cond, home, *blocks):
+        @pl.when(cond)
+        def _():
+            for n in blocks:
+                for e in range(2):
                     for i in range(2):
-                        s2(d, i, home).start()
-
-    s2_start(first_home, True)
+                        s2(n, e, i, home).start()
+
+    s2_start(is_away, True, 0, 1)
+    s2_start(is_home, True, 2)
 
     zmate = z + 1 - 2 * (z % 2)
 
@@ -191,64 +204,56 @@
     a_load.wait()
     own_send(0)
     own_send(1)
-    own_send(2)
 
     wait_into(away, x_r.at[0])
-    s2_start(first_away, False)
-    s2_start([h - f for h, f in zip(homes, first_home)], True)
-    s2_start([1 - h - f for h, f in zip(homes, first_away)], False)
-
-    def piece(d, x_, i):
-        blk, row = place(x_, zl, ((z + d) % 8) // 4, i)
-        return lbuf.at[blk, row, lanes(d)]
+    s2_start(is_home, False, 0, 1)
+    s2_start(is_home, True, 3)
+    s2_start(is_away, False, 2, 3)
+
+    def piece(n, e, x_, i):
+        blk, row = place(x_, zl, (zh + e) % 2, i)
+        return lbuf.at[blk, row, lanes(n)]
 
     xm, xp, xo = (x + 3) % 4, (x + 1) % 4, (x + 2) % 4
 
-    def s3(d, i):
-        return [rcopy(piece(d, x, i), piece(d, x, i), s_s.at[2], s3_r.at[d, 0], at_x(1)),
-                rcopy(piece(d, x, i), piece(d, x, i), s_s.at[2], s3_r.at[d, 1], at_x(3))]
-
-    def s3_relay(d):
-        return [rcopy(piece(d, xm, 0), piece(d, xm, 0), s_s.at[2], s3_r.at[d, 2], at_x(1)),
-                rcopy(piece(d, xp, 1), piece(d, xp, 1), s_s.at[2], s3_r.at[d, 2], at_x(3))]
-
-    GROUPS = ((1, 5), (7, 3), (2, 6), (0, 4))
+    def s3(n, e, i):
+        k = 2 * n + e
+        return [rcopy(piece(n, e, x, i), piece(n, e, x, i), s_s.at[2], s3_r.at[k, 0], at_x(1)),
+                rcopy(piece(n, e, x, i), piece(n, e, x, i), s_s.at[2], s3_r.at[k, 1], at_x(3))]
+
+    def s3_relay(n, e):
+        k = 2 * n + e
+        return [rcopy(piece(n, e, xm, 0), piece(n, e, xm, 0), s_s.at[2], s3_r.at[k, 2], at_x(1)),
+                rcopy(piece(n, e, xp, 1), piece(n, e, xp, 1), s_s.at[2], s3_r.at[k, 2], at_x(3))]
 
     def wait_pair(sem):
         wait_into(lbuf.at[pl.ds(0, 2), pl.ds(0, quart), pl.ds(0, AB)], sem)
 
-    def spread_x(g):
-        for d in GROUPS[g]:
-            wait_pair(s2_r.at[d])
+    def spread_x(n):
+        for e in range(2):
+            wait_pair(s2_r.at[2 * n + e])
             for i in range(2):
-                for cp in s3(d, i):
+                for cp in s3(n, e, i):
                     cp.start()
 
-    def relay_x(g):
-        for d in GROUPS[g]:
-            cps = s3_relay(d)
-            wait_pair(s3_r.at[d, 0])
+    def relay_x(n):
+        for e in range(2):
+            cps = s3_relay(n, e)
+            wait_pair(s3_r.at[2 * n + e, 0])
             cps[0].start()
-            wait_pair(s3_r.at[d, 1])
+            wait_pair(s3_r.at[2 * n + e, 1])
             cps[1].start()
 
-    def wait_x(g):
-        for d in GROUPS[g]:
-            wait_pair(s3_r.at[d, 2])
+    def wait_x(n):
+        for e in range(2):
+            wait_pair(s3_r.at[2 * n + e, 2])
 
     is_end = zl * (3 - zl) == 0
-    at_hi, at_lo = (zl + 1) // 4, (4 - zl) // 4
-
     def cout(m, n):
         return csend.at[n, pl.ds(first[m] + 16 * m, 16 + CHUNKS[m] * AB)]
 
-    def c_copy(m, n):
-        if n == 0:
-            to, slot = zl + 1 - 2 * at_hi, 3 * at_hi
-        elif n == 1:
-            to, slot = zl - 1 + 2 * at_lo, 1 + 2 * at_lo
-        else:
-            to, slot = (zl + 2) % 4, 2
+    def c_copy(m, n, far=False):
+        to, slot = (other[2], 3) if far else (other[n], n)
         t = pl.ds(0, 16 + CHUNKS[m] * AB)
         return rcopy(cout(m, n), crecv.at[m, slot, t], s_s.at[5], c_r.at[m, slot], at_z(zh * 4 + to))
 
@@ -270,6 +275,8 @@
         e = src[0:16, :].astype(jnp.int32).astype(jnp.float32)
         return v * jnp.exp2(e[t:t + 1, :] - 15.0)
 
+    is_inner = zl * (3 - zl) != 0
+
     def compute(m, n0, n1):
         r = mchunk(m)
         n = CHUNKS[m] * AB
@@ -277,32 +284,34 @@
         acc[0:n, ln] = jnp.dot(abuf[0, r, :], lbuf[0, :, ln], preferred_element_type=jnp.float32)
         for yy in range(1, 4):
             acc[0:n, ln] += jnp.dot(abuf[yy, r, :], lbuf[yy, :, ln], preferred_element_type=jnp.float32)
-        for b in range(n0, n1):
-            part = acc[0:n, b * AB:(b + 1) * AB]
-            if b == 3:
-                cown[r, :] = part
-            elif b == 2:
-                ckeep[m, 0:n, :] = part
-                pl.when(is_end)(lambda: send_far(m))
-            else:
-                code(part, cout(m, b))
-                c_copy(m, b).start()
-
-    def send_far(m):
-        code(ckeep[m, 0:CHUNKS[m] * AB, :], cout(m, 2))
-        c_copy(m, 2).start()
+        if n0 == 0:
+            code(acc[0:n, AB:2 * AB], cout(m, 1))
+            pl.when(is_end)(lambda: c_copy(m, 1, True).start())
+            pl.when(is_inner)(lambda: c_copy(m, 1).start())
+            ckeep[m, 0:n, :] = acc[0:n, 0:AB]
+
+            @pl.when(is_end)
+            def _():
+                code(ckeep[m, 0:n, :], cout(m, 0))
+                c_copy(m, 0).start()
+
+        if n0 <= 2 < n1:
+            code(acc[0:n, 2 * AB:3 * AB], cout(m, 2))
+            c_copy(m, 2).start()
+        if n1 == 4:
+            cown[r, :] = acc[0:n, 3 * AB:4 * AB]
 
     def wait_c(m, slot):
         wait_into(crecv.at[m, slot, pl.ds(0, 16 + CHUNKS[m] * AB)], c_r.at[m, slot])
 
     def merge(m):
-        @pl.when(jnp.logical_not(is_end))
+        @pl.when(is_inner)
         def _():
             wait_c(m, 3)
             for t in range(CHUNKS[m]):
                 ckeep[m, t * AB:(t + 1) * AB, :] += decode(crecv.at[m, 3], t)
-            code(ckeep[m, 0:CHUNKS[m] * AB, :], cout(m, 2))
-            c_copy(m, 2).start()
+            code(ckeep[m, 0:CHUNKS[m] * AB, :], cout(m, 0))
+            c_copy(m, 0).start()
 
     def add_slot(m, n):
         wait_c(m, n)
@@ -315,9 +324,9 @@
     def finish_c(m):
         n = CHUNKS[m] * AB
         tot[0:n, :] = cown[mchunk(m), :]
-        pl.when(zl >= 1)(lambda: add_slot(m, 0))
-        pl.when(zl <= 2)(lambda: add_slot(m, 1))
         add_slot(m, 2)
+        pl.when(is_inner)(lambda: add_slot(m, 1))
+        add_slot(m, 0)
         for t in range(CHUNKS[m]):
             at = first[m] + t * AB
             b = at // AB
@@ -345,56 +354,16 @@
         wait_into(abuf.at[:, pl.ds(0, rows * 7 // 8), :], s_s.at[3])
         wait_into(lead.at[:, :, pl.ds(0, 3 * AB)], s_s.at[4])
 
-    spread_x(0)
-    relay_a(0)
-    spread_x(1)
-    relay_x(0)
-    relay_a(1)
-    own_send(3)
-    own_send(4)
-    relay_x(1)
-    spread_x(2)
-    spread_x(3)
-    send_lead()
-    relay_a(2)
-    finish_a(0)
-    wait_x(0)
-    wait_x(1)
-    wait_a(0)
-    compute(0, 0, 2)
-    relay_x(2)
-    finish_a(1)
-    wait_a(1)
-    compute(1, 0, 2)
-    relay_x(3)
-    relay_a(3)
-    wait_x(2)
-    wait_x(3)
-    compute(0, 2, 4)
-    relay_a(4)
-    fwd_lead()
-    compute(1, 2, 4)
-    finish_a(2)
-    merge(0)
-    wait_a(2)
-    compute(2, 0, 4)
-    finish_a(3)
-    merge(1)
-    finish_a(4)
-    wait_a(3)
-    compute(3, 0, 4)
-    wait_a(4)
-    compute(4, 0, 4)
-    wait_lead()
-    merge(2)
-    sent()
-    finish_c(0)
-    merge(3)
-    finish_c(1)
-    merge(4)
-    finish_c(2)
-    finish_c(3)
-    finish_c(4)
+    steps = {f.__name__: f for f in (
+        spread_x, relay_x, wait_x, own_send, relay_a, finish_a, wait_a, send_lead, fwd_lead, wait_lead,
+        compute, merge, sent, finish_c)}
+
+    def run(plan):
+        for name, *at in plan:
+            steps[name](*at)
+
+    run(FIRST)
+    run(REST)
     wait_into(csend, s_s.at[5])
 
     lrows = diag_ref.shape[0]

time: 92.6 us -> 83.4 us (0.901)
  the two profiles are of different devices: /device:TPU:8 before, /device:TPU:57 now
where the time goes in v4:
time: 83.4 us; the launch traced here: 82.6 us
  Pallas kernels  78.8 us (94%)
  local copies, waits for them, and re-layouts  3.14 us (4%)
    pallas_call x1, Pallas kernels, per_device(): pl.pallas_call(kernel, out_shape=(jax.ShapeDtypeStruct((cols, rows), bf),...  78.8 us
    unnamed x2, local copies, waits for them, and re-layouts  3.14 us

profile of v4, /device:TPU:57, one launch (start us, length us, event | category | flops | bytes accessed | tf_op | source)
XLA Modules:
  0.0 82.6 jit_solution(15315487899444374669)
XLA Ops:
  0.6 78.8 %shard_map.68 = (bf16[128,1536]{1,0:T(8,128)(2,1)}, f32[64,128]{1,0:T(8,128)}) custom-call(bf16[1536,384]{1,0:T(8,128)(2,1)} %a_ref.1, bf16[1536,128]{1,0:T(8,128)(2,1)} %l_ref.1, f32[64,128]{1,0:T(8,128)} %piv_ref.1, s32[8]{0:T(128)} %sn_ref.1, s32[8,48]{1,0:T(8,128)} %anc_ref.1), custom_call_target="tpu_custom_call" | custom-call | flops 5000000000 | bytes 4000000 | tf_op jit(solution)/shard_map/pallas_call | solution.py:401
  79.4 1.8 %copy.9 = bf16[128,1536]{1,0:T(8,128)(2,1)} copy(bf16[128,1536]{1,0:T(8,128)(2,1)} %get-tuple-element.4) | data formatting | bytes 786432
  81.2 1.4 %copy.10 = f32[64,128]{1,0:T(8,128)} copy(f32[64,128]{1,0:T(8,128)} %get-tuple-element.5) | data formatting | bytes 65536

commit v5 on v4

--- a/solution.py
+++ b/solution.py
@@ -281,9 +281,9 @@
         r = mchunk(m)
         n = CHUNKS[m] * AB
         ln = pl.ds(n0 * AB, (n1 - n0) * AB)
-        acc[0:n, ln] = jnp.dot(abuf[0, r, :], lbuf[0, :, ln], preferred_element_type=jnp.float32)
-        for yy in range(1, 4):
-            acc[0:n, ln] += jnp.dot(abuf[yy, r, :], lbuf[yy, :, ln], preferred_element_type=jnp.float32)
+        a = jnp.concatenate([abuf[yy, r, :] for yy in range(4)], axis=1)
+        b = lbuf[:, :, ln].reshape(4 * lbuf.shape[1], (n1 - n0) * AB)
+        acc[0:n, ln] = jnp.dot(a, b, preferred_element_type=jnp.float32)
         if n0 == 0:
             code(acc[0:n, AB:2 * AB], cout(m, 1))
             pl.when(is_end)(lambda: c_copy(m, 1, True).start())

time: 83.4 us -> 82.1 us (0.984)
  Pallas kernels: 78.8 us -> 77.7 us
    pallas_call x1, Pallas kernels: 78.8 us -> 77.7 us  [per_device(): pl.pallas_call(kernel, out_shape=(jax.ShapeDtypeStruct((cols, rows), bf),...]
where the time goes in v5:
time: 82.1 us; the launch traced here: 81.5 us
  Pallas kernels  77.7 us (95%)
  local copies, waits for them, and re-layouts  3.14 us (4%)
    pallas_call x1, Pallas kernels, per_device(): pl.pallas_call(kernel, out_shape=(jax.ShapeDtypeStruct((cols, rows), bf),...  77.7 us
    unnamed x2, local copies, waits for them, and re-layouts  3.14 us

profile of v5, /device:TPU:57, one launch (start us, length us, event | category | flops | bytes accessed | tf_op | source)
XLA Modules:
  0.0 81.5 jit_solution(3714987866926240274)
XLA Ops:
  0.6 77.7 %shard_map.68 = (bf16[128,1536]{1,0:T(8,128)(2,1)}, f32[64,128]{1,0:T(8,128)}) custom-call(bf16[1536,384]{1,0:T(8,128)(2,1)} %a_ref.1, bf16[1536,128]{1,0:T(8,128)(2,1)} %l_ref.1, f32[64,128]{1,0:T(8,128)} %piv_ref.1, s32[8]{0:T(128)} %sn_ref.1, s32[8,48]{1,0:T(8,128)} %anc_ref.1), custom_call_target="tpu_custom_call" | custom-call | flops 5000000000 | bytes 4000000 | tf_op jit(solution)/shard_map/pallas_call | solution.py:401
  78.3 1.8 %copy.9 = bf16[128,1536]{1,0:T(8,128)(2,1)} copy(bf16[128,1536]{1,0:T(8,128)(2,1)} %get-tuple-element.4) | data formatting | bytes 786432
  80.1 1.4 %copy.10 = f32[64,128]{1,0:T(8,128)} copy(f32[64,128]{1,0:T(8,128)} %get-tuple-element.5) | data formatting | bytes 65536

commit v6 on v5

--- a/solution.py
+++ b/solution.py
@@ -8,22 +8,22 @@
 AB = 128
 W = 512
 MESH = pl.DeviceIdType.MESH
-CHUNKS = (3, 3, 3, 2, 1)
+CHUNKS = (3, 3, 3, 3)
 MCH = len(CHUNKS)
 TOP = max(CHUNKS)
 
 FIRST = (
     ("spread_x", 0), ("relay_a", 0), ("own_send", 2), ("spread_x", 1), ("relay_x", 0), ("send_lead",), ("relay_a", 1),
-    ("own_send", 3), ("own_send", 4), ("relay_x", 1), ("spread_x", 2), ("finish_a", 0), ("relay_a", 2),
+    ("own_send", 3), ("relay_x", 1), ("spread_x", 2), ("finish_a", 0), ("relay_a", 2),
 )
 REST = (
-    ("wait_x", 0), ("wait_x", 1), ("spread_x", 3), ("wait_a", 0), ("compute", 0, 0, 2), ("relay_x", 2), ("finish_a", 1),
-    ("wait_a", 1), ("compute", 1, 0, 2), ("merge", 0), ("relay_x", 3), ("relay_a", 3), ("relay_a", 4),
+    ("wait_x", 0), ("wait_x", 1), ("spread_x", 3), ("wait_a", 0), ("compute", 0, 0, 2), ("finish_a", 1), ("relay_x", 2),
+    ("wait_a", 1), ("compute", 1, 0, 2), ("merge", 0), ("relay_x", 3), ("relay_a", 3),
     ("wait_x", 2), ("compute", 0, 2, 3), ("finish_a", 2), ("merge", 1), ("fwd_lead",),
-    ("wait_x", 3), ("wait_a", 2), ("compute", 2, 0, 4), ("finish_a", 3), ("finish_a", 4),
-    ("wait_a", 3), ("compute", 3, 0, 4), ("merge", 2), ("wait_a", 4), ("compute", 4, 0, 4), ("compute", 1, 2, 4), ("compute", 0, 3, 4),
-    ("wait_lead",), ("sent",), ("merge", 3), ("finish_c", 0), ("merge", 4),
-    ("finish_c", 1), ("finish_c", 2), ("finish_c", 3), ("finish_c", 4),
+    ("wait_x", 3), ("wait_a", 2), ("compute", 2, 0, 4), ("finish_a", 3),
+    ("wait_a", 3), ("compute", 3, 0, 4), ("merge", 2), ("compute", 1, 2, 4), ("compute", 0, 3, 4),
+    ("wait_lead",), ("sent",), ("merge", 3), ("finish_c", 0),
+    ("finish_c", 1), ("finish_c", 2), ("finish_c", 3),
 )
 
 
@@ -65,23 +65,8 @@
             src_ref=src, dst_ref=dst, send_sem=ssem, recv_sem=rsem,
             device_id=device, device_id_type=MESH)
 
-    barrier = pltpu.get_barrier_semaphore()
-    partners = [at_z((z + d) % 8) for d in range(1, 8)]
-    partners += [dev((x + d) % 4, y, ((zh + e) % 2) * 4 + zl, c)
-                 for d in range(1, 4) for e in range(2)]
-    partners += [at_y(1), at_y(3), sib]
-    for partner in partners:
-        pl.semaphore_signal(barrier, inc=1, device_id=partner, device_id_type=MESH)
-
-    def mchunk(m):
-        return pl.ds(first[m], CHUNKS[m] * AB)
-
-    def mhalves(m):
-        n = CHUNKS[m] * AB // 2
-        return pl.ds(first[m], n), pl.ds(first[m] + n, n)
-
     def ablk(y_, c_, r):
-        return abuf.at[y_, r, pl.ds(pl.multiple_of(c_ * kw, 128), kw)]
+        return abuf.at[y_, c_, r, :]
 
     a_load = pltpu.make_async_copy(a_ref, ablk(y, c, pl.ds(0, rows)), in_sem.at[3])
     l_load = pltpu.make_async_copy(l_ref, l_in, in_sem.at[0])
@@ -91,6 +76,21 @@
     anc_load.start()
     a_load.start()
     piv_load.start()
+
+    barrier = pltpu.get_barrier_semaphore()
+    partners = [at_z((z + d) % 8) for d in range(1, 8)]
+    partners += [dev((x + d) % 4, y, ((zh + e) % 2) * 4 + zl, c)
+                 for d in range(1, 4) for e in range(2)]
+    partners += [at_y(1), at_y(3), sib]
+    for partner in partners:
+        pl.semaphore_signal(barrier, inc=1, device_id=partner, device_id_type=MESH)
+
+    def mchunk(m):
+        return pl.ds(first[m], CHUNKS[m] * AB)
+
+    def mhalves(m):
+        n = CHUNKS[m] * AB // 2
+        return pl.ds(first[m], n), pl.ds(first[m] + n, n)
 
     l_load.wait()
     anc_load.wait()
@@ -112,9 +112,6 @@
     for cp in s1:
         cp.start()
 
-    def lanes(n):
-        return pl.ds(n * AB, AB)
-
     def place(x_, zl_, zh_, i):
         home = 1 - (x_ + zl_ // 2) % 2
         xs = home * (x_ // 2) + (1 - home) * (((x_ + 3 + 2 * i) % 4) // 2)
@@ -125,7 +122,7 @@
         tz = other[n]
         src = lhat.at[tz % 2, pl.ds(i * quart, quart), :] if home else away.at[i, tz % 2]
         blk, row = place(x, tz, zh, i)
-        dst = lbuf.at[blk, row, lanes(n)]
+        dst = lbuf.at[n, blk, row]
         sem = s2_r.at[2 * n + e]
         if n == 3 and e == 0:
             return pltpu.make_async_copy(src, dst, sem)
@@ -148,7 +145,7 @@
     zmate = z + 1 - 2 * (z % 2)
 
     def hblk(zb, cb):
-        return lead.at[:, :, pl.ds(pl.multiple_of(((zb % 2) * 2 + cb) * AB, 128), AB)]
+        return lead.at[(zb % 2) * 2 + cb]
 
     h_own = [rcopy(lhat, hblk(z, c), s_s.at[4], h_r.at[0], at_z(zmate)),
              rcopy(lhat, hblk(z, c), s_s.at[4], h_r.at[1], sib)]
@@ -189,17 +186,17 @@
             cp.start()
 
     def relay_a(m):
-        wait_into(abuf.at[pl.ds(0, 2), mchunk(m), pl.ds(0, kw)], a_r.at[m, 0])
+        wait_into(abuf.at[0, :, mchunk(m), :], a_r.at[m, 0])
         for cp in a_fwd(m):
             cp.start()
 
     def finish_a(m):
-        wait_into(abuf.at[0, mchunk(m), pl.ds(0, kw)], a_r.at[m, 1])
+        wait_into(abuf.at[0, 0, mchunk(m), :], a_r.at[m, 1])
         for cp in a_opp(m):
             cp.start()
 
     def wait_a(m):
-        wait_into(abuf.at[:, mchunk(m), pl.ds(0, kw)], ab_r.at[m])
+        wait_into(abuf.at[:, 0, mchunk(m), :], ab_r.at[m])
 
     a_load.wait()
     own_send(0)
@@ -212,7 +209,7 @@
 
     def piece(n, e, x_, i):
         blk, row = place(x_, zl, (zh + e) % 2, i)
-        return lbuf.at[blk, row, lanes(n)]
+        return lbuf.at[n, blk, row]
 
     xm, xp, xo = (x + 3) % 4, (x + 1) % 4, (x + 2) % 4
 
@@ -227,7 +224,7 @@
                 rcopy(piece(n, e, xp, 1), piece(n, e, xp, 1), s_s.at[2], s3_r.at[k, 2], at_x(3))]
 
     def wait_pair(sem):
-        wait_into(lbuf.at[pl.ds(0, 2), pl.ds(0, quart), pl.ds(0, AB)], sem)
+        wait_into(lbuf.at[0, pl.ds(0, 2), pl.ds(0, quart)], sem)
 
     def spread_x(n):
         for e in range(2):
@@ -281,8 +278,8 @@
         r = mchunk(m)
         n = CHUNKS[m] * AB
         ln = pl.ds(n0 * AB, (n1 - n0) * AB)
-        a = jnp.concatenate([abuf[yy, r, :] for yy in range(4)], axis=1)
-        b = lbuf[:, :, ln].reshape(4 * lbuf.shape[1], (n1 - n0) * AB)
+        a = jnp.concatenate([abuf[yy, cc, r, :] for yy in range(4) for cc in range(2)], axis=1)
+        b = jnp.concatenate([lbuf[j].reshape(8 * kw, AB) for j in range(n0, n1)], axis=1)
         acc[0:n, ln] = jnp.dot(a, b, preferred_element_type=jnp.float32)
         if n0 == 0:
             code(acc[0:n, AB:2 * AB], cout(m, 1))
@@ -334,14 +331,13 @@
             abf[t * AB:(t + 1) * AB, :] = v.astype(jnp.bfloat16)
             out_v[:, at:at + AB] = v.T.astype(jnp.bfloat16)
         out_copy(m).start()
-        part = lax.dot_general(
-            lead[first[m] // half, pl.ds(first[m] % half, n), :], abf[0:n, :],
-            (((0,), (0,)), ((), ())), preferred_element_type=jnp.float32)
+        lhs = jnp.concatenate([lead[j, first[m] // half, pl.ds(first[m] % half, n), :] for j in range(4)], axis=1)
+        part = lax.dot_general(lhs, abf[0:n, :], (((0,), (0,)), ((), ())), preferred_element_type=jnp.float32)
         corr[...] = part if m == 0 else corr[...] + part
 
     def wait_lead():
         h_loc.wait()
-        wait_into(lead.at[:, :, pl.ds(0, 2 * AB)], h_r.at[1])
+        wait_into(lead.at[pl.ds(0, 2)], h_r.at[1])
 
     def fwd_lead():
         wait_into(hblk(zmate, c), h_r.at[0])
@@ -349,10 +345,10 @@
 
     def sent():
         wait_into(away, s_s.at[0])
-        wait_into(abuf.at[0, pl.ds(0, 14 * quart * AB // (2 * kw)), :], s_s.at[1])
+        wait_into(abuf.at[0, 0, pl.ds(0, 14 * quart * AB // kw), :], s_s.at[1])
         wait_into(abuf.at[0], s_s.at[2])
-        wait_into(abuf.at[:, pl.ds(0, rows * 7 // 8), :], s_s.at[3])
-        wait_into(lead.at[:, :, pl.ds(0, 3 * AB)], s_s.at[4])
+        wait_into(abuf.at[:, :, pl.ds(0, rows * 7 // 8), :], s_s.at[3])
+        wait_into(lead.at[pl.ds(0, 3)], s_s.at[4])
 
     steps = {f.__name__: f for f in (
         spread_x, relay_x, wait_x, own_send, relay_a, finish_a, wait_a, send_lead, fwd_lead, wait_lead,
@@ -371,7 +367,7 @@
     def mine(p_):
         return pl.ds(pl.multiple_of(p_ * lrows, lrows), lrows)
 
-    for d in (4, 1, 3, 2, 5, 7, 6):
+    for d in (6, 5, 7, 4, 2, 1, 3):
         to = (zh + d // 4) % 2 * 4 + (x + d) % 4
         code(corr[mine(to), :], dsend.at[d - 1], lrows)
         cp = rcopy(dsend.at[d - 1], drecv.at[d - 1], s_s.at[6], x_r.at[1], (to, q))
@@ -405,14 +401,14 @@
         in_specs=[anys, anys, anys, pl.BlockSpec(memory_space=pltpu.SMEM), anys],
         out_specs=(anys, anys),
         scratch_shapes=[
-            vm((4, rows, 2 * kw), bf),
+            vm((4, 2, rows, kw), bf),
             vm((rows, cols), bf),
             vm((lrows, cols), f32),
             vm(anc_list.shape, jnp.int32),
             vm((2, rows // 2, cols), bf),
             vm((2, 2, rows // 8, cols), bf),
-            vm((4, 2 * kw, 4 * cols), bf),
-            vm((2, rows // 2, W), bf),
+            vm((4, 4, 2 * kw, cols), bf),
+            vm((4, 2, rows // 2, cols), bf),
             vm((16, cols), f32),
             vm((TOP * AB, 4 * cols), f32),
             vm((rows, cols), f32),

time: 82.1 us -> 81.6 us (level)
  no operation moved by 1% of the time
where the time goes in v6:
time: 81.6 us; the launch traced here: 81.4 us
  Pallas kernels  77.6 us (95%)
  local copies, waits for them, and re-layouts  3.14 us (4%)
    pallas_call x1, Pallas kernels, per_device(): pl.pallas_call(kernel, out_shape=(jax.ShapeDtypeStruct((cols, rows), bf),...  77.6 us
    unnamed x2, local copies, waits for them, and re-layouts  3.14 us

profile of v6, /device:TPU:57, one launch (start us, length us, event | category | flops | bytes accessed | tf_op | source)
XLA Modules:
  0.0 81.4 jit_solution(16429033576159296498)
XLA Ops:
  0.6 77.6 %shard_map.68 = (bf16[128,1536]{1,0:T(8,128)(2,1)}, f32[64,128]{1,0:T(8,128)}) custom-call(bf16[1536,384]{1,0:T(8,128)(2,1)} %a_ref.1, bf16[1536,128]{1,0:T(8,128)(2,1)} %l_ref.1, f32[64,128]{1,0:T(8,128)} %piv_ref.1, s32[8]{0:T(128)} %sn_ref.1, s32[8,48]{1,0:T(8,128)} %anc_ref.1), custom_call_target="tpu_custom_call" | custom-call | flops 5000000000 | bytes 4000000 | tf_op jit(solution)/shard_map/pallas_call | solution.py:397
  78.3 1.8 %copy.9 = bf16[128,1536]{1,0:T(8,128)(2,1)} copy(bf16[128,1536]{1,0:T(8,128)(2,1)} %get-tuple-element.4) | data formatting | bytes 786432
  80.0 1.4 %copy.10 = f32[64,128]{1,0:T(8,128)} copy(f32[64,128]{1,0:T(8,128)} %get-tuple-element.5) | data formatting | bytes 65536

commit v7 on v6

--- a/solution.py
+++ b/solution.py
@@ -23,13 +23,13 @@
     ("wait_x", 3), ("wait_a", 2), ("compute", 2, 0, 4), ("finish_a", 3),
     ("wait_a", 3), ("compute", 3, 0, 4), ("merge", 2), ("compute", 1, 2, 4), ("compute", 0, 3, 4),
     ("wait_lead",), ("sent",), ("merge", 3), ("finish_c", 0),
-    ("finish_c", 1), ("finish_c", 2), ("finish_c", 3),
+    ("finish_c", 2), ("finish_c", 3), ("finish_c", 1),
 )
 
 
 def kernel(
     a_ref, l_ref, piv_ref, sn_ref, anc_ref, out_ref, diag_ref,
-    abuf, l_in, piv, anc, lhat, away, lbuf, lead, live, acc, cown, csend, crecv, ckeep, tot, abf, corr, dsend, drecv, out_v, diag_v,
+    abuf, l_in, piv, anc, lhat, away, lbuf, lead, live, acc, cown, csend, crecv, ckeep, abf, corr, dsend, drecv, out_v, diag_v,
     in_sem, s_s, x_r, s2_r, s3_r, a_r, ab_r, c_r, h_r, out_s,
 ):
     rows = l_ref.shape[0]
@@ -313,24 +313,28 @@
     def add_slot(m, n):
         wait_c(m, n)
         for t in range(CHUNKS[m]):
-            tot[t * AB:(t + 1) * AB, :] += decode(crecv.at[m, n], t)
+            cown[first[m] + t * AB:first[m] + (t + 1) * AB, :] += decode(crecv.at[m, n], t)
 
     def out_copy(m):
         return pltpu.make_async_copy(out_v.at[:, mchunk(m)], out_ref.at[:, mchunk(m)], out_s.at[0])
 
+    def value(m, t):
+        at = first[m] + t * AB
+        return -(cown[at:at + AB, :] * live[at // AB:at // AB + 1, :])
+
+    def store_out(m):
+        for t in range(CHUNKS[m]):
+            at = first[m] + t * AB
+            out_v[:, at:at + AB] = value(m, t).T.astype(jnp.bfloat16)
+        out_copy(m).start()
+
     def finish_c(m):
         n = CHUNKS[m] * AB
-        tot[0:n, :] = cown[mchunk(m), :]
         add_slot(m, 2)
         pl.when(is_inner)(lambda: add_slot(m, 1))
         add_slot(m, 0)
         for t in range(CHUNKS[m]):
-            at = first[m] + t * AB
-            b = at // AB
-            v = -(tot[t * AB:(t + 1) * AB, :] * live[b:b + 1, :])
-            abf[t * AB:(t + 1) * AB, :] = v.astype(jnp.bfloat16)
-            out_v[:, at:at + AB] = v.T.astype(jnp.bfloat16)
-        out_copy(m).start()
+            abf[t * AB:(t + 1) * AB, :] = value(m, t).astype(jnp.bfloat16)
         lhs = jnp.concatenate([lead[j, first[m] // half, pl.ds(first[m] % half, n), :] for j in range(4)], axis=1)
         part = lax.dot_general(lhs, abf[0:n, :], (((0,), (0,)), ((), ())), preferred_element_type=jnp.float32)
         corr[...] = part if m == 0 else corr[...] + part
@@ -372,6 +376,8 @@
         code(corr[mine(to), :], dsend.at[d - 1], lrows)
         cp = rcopy(dsend.at[d - 1], drecv.at[d - 1], s_s.at[6], x_r.at[1], (to, q))
         cp.start()
+    for m in range(MCH):
+        store_out(m)
     total = corr[mine(p), :]
     wait_into(drecv, x_r.at[1])
     for d in range(1, 8):
@@ -415,7 +421,6 @@
             vm((3, rows + 16 * MCH, cols), jnp.int16),
             vm((MCH, 4, 16 + TOP * AB, cols), jnp.int16),
             vm((MCH, TOP * AB, cols), f32),
-            vm((TOP * AB, cols), f32),
             vm((TOP * AB, cols), bf),
             vm((W, cols), f32),
             vm((7, lrows + 16, cols), jnp.int16),

time: 81.6 us -> 81.5 us (level)
  no operation moved by 1% of the time
where the time goes in v7:
time: 81.5 us; the launch traced here: 81.3 us
  Pallas kernels  77.5 us (95%)
  local copies, waits for them, and re-layouts  3.14 us (4%)
    pallas_call x1, Pallas kernels, per_device(): pl.pallas_call(kernel, out_shape=(jax.ShapeDtypeStruct((cols, rows), bf),...  77.5 us
    unnamed x2, local copies, waits for them, and re-layouts  3.14 us

profile of v7, /device:TPU:57, one launch (start us, length us, event | category | flops | bytes accessed | tf_op | source)
XLA Modules:
  0.0 81.3 jit_solution(4491956040264470913)
XLA Ops:
  0.6 77.5 %shard_map.68 = (bf16[128,1536]{1,0:T(8,128)(2,1)}, f32[64,128]{1,0:T(8,128)}) custom-call(bf16[1536,384]{1,0:T(8,128)(2,1)} %a_ref.1, bf16[1536,128]{1,0:T(8,128)(2,1)} %l_ref.1, f32[64,128]{1,0:T(8,128)} %piv_ref.1, s32[8]{0:T(128)} %sn_ref.1, s32[8,48]{1,0:T(8,128)} %anc_ref.1), custom_call_target="tpu_custom_call" | custom-call | flops 5000000000 | bytes 4000000 | tf_op jit(solution)/shard_map/pallas_call | solution.py:403
  78.2 1.8 %copy.9 = bf16[128,1536]{1,0:T(8,128)(2,1)} copy(bf16[128,1536]{1,0:T(8,128)(2,1)} %get-tuple-element.4) | data formatting | bytes 786432
  80.0 1.4 %copy.10 = f32[64,128]{1,0:T(8,128)} copy(f32[64,128]{1,0:T(8,128)} %get-tuple-element.5) | data formatting | bytes 65536

commit v8 on v7

--- a/solution.py
+++ b/solution.py
@@ -23,8 +23,9 @@
     ("wait_x", 3), ("wait_a", 2), ("compute", 2, 0, 4), ("finish_a", 3),
     ("wait_a", 3), ("compute", 3, 0, 4), ("merge", 2), ("compute", 1, 2, 4), ("compute", 0, 3, 4),
     ("wait_lead",), ("sent",), ("merge", 3), ("finish_c", 0),
-    ("finish_c", 2), ("finish_c", 3), ("finish_c", 1),
 )
+INNER = (("finish_c", 2), ("finish_c", 3), ("finish_c", 1))
+END = (("finish_c", 1), ("finish_c", 2), ("finish_c", 3))
 
 
 def kernel(
@@ -364,6 +365,8 @@
 
     run(FIRST)
     run(REST)
+    pl.when(is_inner)(lambda: run(INNER))
+    pl.when(is_end)(lambda: run(END))
     wait_into(csend, s_s.at[5])
 
     lrows = diag_ref.shape[0]

time: 81.5 us -> 81.3 us (level)
  no operation moved by 1% of the time
where the time goes in v8:
time: 81.3 us; the launch traced here: 80.8 us
  Pallas kernels  77.1 us (95%)
  local copies, waits for them, and re-layouts  3.14 us (4%)
    pallas_call x1, Pallas kernels, per_device(): pl.pallas_call(kernel, out_shape=(jax.ShapeDtypeStruct((cols, rows), bf),...  77.1 us
    unnamed x2, local copies, waits for them, and re-layouts  3.14 us

profile of v8, /device:TPU:57, one launch (start us, length us, event | category | flops | bytes accessed | tf_op | source)
XLA Modules:
  0.0 80.8 jit_solution(10860989455691360098)
XLA Ops:
  0.6 77.1 %shard_map.68 = (bf16[128,1536]{1,0:T(8,128)(2,1)}, f32[64,128]{1,0:T(8,128)}) custom-call(bf16[1536,384]{1,0:T(8,128)(2,1)} %a_ref.1, bf16[1536,128]{1,0:T(8,128)(2,1)} %l_ref.1, f32[64,128]{1,0:T(8,128)} %piv_ref.1, s32[8]{0:T(128)} %sn_ref.1, s32[8,48]{1,0:T(8,128)} %anc_ref.1), custom_call_target="tpu_custom_call" | custom-call | flops 5000000000 | bytes 4000000 | tf_op jit(solution)/shard_map/pallas_call | solution.py:406
  77.7 1.8 %copy.9 = bf16[128,1536]{1,0:T(8,128)(2,1)} copy(bf16[128,1536]{1,0:T(8,128)(2,1)} %get-tuple-element.4) | data formatting | bytes 786432
  79.5 1.4 %copy.10 = f32[64,128]{1,0:T(8,128)} copy(f32[64,128]{1,0:T(8,128)} %get-tuple-element.5) | data formatting | bytes 65536
